TPU v7x, 512 devices: a whole 4x4x16 slice. The times are simulated.
512 devices in a mesh: harm: 64 (over y, z), grp: 8 (over x, core).
Axes of the slice: x: 4, y: 4, z: 16, core: 2. Of those that a mesh axis runs over, the one named last changes fastest.
Arguments:
- vectors: float32 [128, 16, 65536], P('harm', None, 'grp'), may hold values from -6 to 6
- stiffness: float32 [65536], P('grp'), may hold values from 0.5 to 4
- attach: int32 [8192], P('grp'), may hold values from 0 to 8191, as said below
- live: int32 [8], P('grp'), may hold values from 512 to 1024
- pair_harm: int32 [64], replicated, may hold values from 0 to 63, each once
- mistune: float32 [128, 8, 1024], P(None, 'grp'), may hold values from 0.5 to 2
Outputs:
- image: float32 [128, 16, 65536], P('harm', None, 'grp')
- gram: float32 [2, 16, 16], replicated
Inputs may be any that keep to these rules, and one draw needn't show every extreme that they name: `attach`: within each block of 1024 rows of one grp index the entries are distinct.
All inputs are finite; a program needn't handle non-finite values.
Results may differ from a plain program's by a relative error of at most 0.00005.
Values sent between devices are 32-bit elements; how exact they have to be, the bound alone decides.
No kernel may reach another device: no remote copies, remote signals or barrier semaphores. Data moves between devices by JAX's collectives and lax.ppermute only.
A program may use at most 64 MiB of HBM per device.

v0:
```python
import math

import jax
import jax.numpy as jnp
from jax import lax
from jax.sharding import PartitionSpec as P


def extended(cells, sides, width):
    for axis, dim in sides:
        count = lax.axis_size(axis)
        ends = count - 1
        head = lax.slice_in_dim(cells, 0, width, axis=dim)
        tail = lax.slice_in_dim(cells, cells.shape[dim] - width, cells.shape[dim], axis=dim)
        cells = jnp.concatenate(
            [
                lax.ppermute(tail, axis, [(i, (i + 1) % count) for i in range(ends)]),
                cells,
                lax.ppermute(head, axis, [((i + 1) % count, i) for i in range(ends)]),
            ],
            axis=dim,
        )
    return cells


def partner_2(block, axis, distance):
    count = lax.axis_size(axis)
    route = []
    for low in range(count):
        high = low | 1 << distance
        if high != low and high < count:
            route += [(low, high), (high, low)]
    return lax.ppermute(block, axis, route)


def slot_tables(pair_harm, slots, blades):
    half = blades // 2
    onehot = (slots % half)[:, None] == jnp.arange(half, dtype=jnp.int32)[None, :]
    harmonic = jnp.sum(jnp.where(onehot, pair_harm[None, :], 0), axis=1)
    imag = slots >= half
    theta = jnp.where(
        harmonic == 0,
        jnp.where(imag, math.pi, 0.0),
        2.0 * math.pi * harmonic.astype(jnp.float32) / blades,
    )
    coup = jnp.where(harmonic == 0, 0.0, jnp.where(imag, -1.0, 1.0) * jnp.sin(theta))
    return (theta, coup, harmonic, imag)


def basis_table(theta, harmonic, imag, blades):
    blade_ids = jnp.arange(blades, dtype=jnp.float32)
    angle = blade_ids[:, None] * theta[None, :]
    wide = math.sqrt(2.0 / blades) * jnp.where(imag[None, :], jnp.sin(angle), jnp.cos(angle))
    return jnp.where(harmonic[None, :] == 0, jnp.cos(angle) / math.sqrt(blades), wide)


def local(vectors, stiffness, attach, live, pair_harm, mistune):
    blades = pair_harm.shape[0] * 2
    slot_count = vectors.shape[0]
    row_count = attach.shape[0]
    harm_size = lax.axis_size("harm")
    first_slot = lax.axis_index("harm") * slot_count
    own_slots = first_slot + jnp.arange(slot_count, dtype=jnp.int32)
    theta, coup, harmonic, imag = slot_tables(pair_harm, own_slots, blades)
    edges = jnp.concatenate([vectors[:, :, :1], vectors[:, :, -1:]], axis=2)
    widened = extended(edges, (("grp", 2),), 1)
    padded = jnp.concatenate([widened[:, :, :1], vectors, widened[:, :, -1:]], axis=2)
    partner = partner_2(padded, "harm", harm_size.bit_length() - 2)
    diag = 2.0 + stiffness[None, None, :] + 2.0 * (1.0 - jnp.cos(theta))[:, None, None]
    adjusted = (
        diag * vectors
        - padded[:, :, :-2]
        - padded[:, :, 2:]
        + coup[:, None, None] * (partner[:, :, 2:] - partner[:, :, :-2])
    )
    alive = (jnp.arange(row_count, dtype=jnp.int32) < live[0]).astype(jnp.float32)
    rows = jnp.take(vectors, attach, axis=2) * alive[None, None, :]
    all_slots = jnp.arange(blades, dtype=jnp.int32)
    theta_all, coup_all, harmonic_all, imag_all = slot_tables(pair_harm, all_slots, blades)
    basis = basis_table(theta_all, harmonic_all, imag_all, blades)
    stiff_rows = mistune[:, 0, :]
    blade = jnp.einsum(
        "bk,kvr->bvr",
        basis,
        lax.all_gather(rows, "harm", axis=0, tiled=True),
        precision=lax.Precision.HIGHEST,
    )
    forced = stiff_rows[:, None, :] * blade
    own_basis = lax.dynamic_slice_in_dim(basis, first_slot, slot_count, 1)
    back = jnp.einsum("bk,bvr->kvr", own_basis, forced, precision=lax.Precision.HIGHEST)
    back = back * alive[None, None, :]
    image = adjusted.at[:, :, attach].add(back)
    first = jnp.einsum("kvs,kws->vw", vectors, image, precision=lax.Precision.HIGHEST)
    second = jnp.einsum("kvs,kws->vw", image, image, precision=lax.Precision.HIGHEST)
    first, second = lax.psum((first, second), ("harm", "grp"))
    return (image, jnp.stack([first, second]))


def solution(mesh):
    in_specs = (P("harm", None, "grp"), P("grp"), P("grp"), P("grp"), P(), P(None, "grp", None))
    out_specs = (P("harm", None, "grp"), P())
    return jax.shard_map(local, mesh=mesh, in_specs=in_specs, out_specs=out_specs, check_vma=False)
```

profile of v0, /device:TPU:1, one launch (start us, length us, event | category | flops | bytes accessed | tf_op | source)
XLA Modules:
  0.0 436.0 jit_solution(5100554374800999819)
XLA Ops:
  7.2 0.0 copy-start
  7.2 0.0 copy-start.3
  7.2 0.0 copy-start.2
  7.2 0.0 all-gather.2.cloned.1.call-start
  8.0 0.7 broadcast_clamp_fusion
  8.7 0.7 fusion.16
  9.4 9.9 %copy.75 = f32[2,16,8192]{1,0,2:T(2,128)} copy(f32[2,16,8192]{2,1,0:T(8,128)} %param.6) | data formatting | bytes 2097152 | tf_op args[0]
  19.2 6.9 %gather_fusion = f32[1024,2,16]{2,1,0:T(2,128)S(1)} fusion(f32[2,16,8192]{1,0,2:T(2,128)} %copy.75, s32[1024]{0:T(1024)S(1)} %get-tuple-element.16), kind=kCustom, calls=%fused_computation | custom fusion | bytes 266240 | tf_op jit(solution)/shard_map/jit(_take)/gather | solution.py:77
  26.2 4.9 %multiply_bitcast_fusion = f32[2,16,1024]{1,0,2:T(2,128)S(1)} fusion(f32[1024,2,16]{2,1,0:T(2,128)S(1)} %gather_fusion, pred[1024]{0:T(1024)(128)(4,1)S(1)} %get-tuple-element.21, f32[1024]{0:T(1024)S(1)} %get-tuple-element.20), kind=kLoop, calls=%fused_computation.18 | loop fusion | flops 65536 | bytes 267264 | tf_op jit(solution)/shard_map/mul | solution.py:77
  31.1 1.1 copy.76
  32.1 0.0 all-gather.2.cloned.1.call-update
  32.2 0.0 copy-done
  32.2 0.1 fusion.25
  32.2 4.5 %collective-permute-start = (f32[2,16,1]{2,1,0:T(8,128)S(1)}, f32[2,16,1]{2,1,0:T(8,128)S(1)}, u32[]{:S(2)}, u32[]{:S(2)}) collective-permute-start(f32[2,16,1]{2,1,0:T(8,128)S(1)} %get-tuple-element.15), channel_id=1, source_target_pairs={{0,1},{1,2},{2,3},{3,4},{4,5},{5,6},{6,7},{8,9},{9,10},{10,11},{11... | collective-permute-start | bytes 392 | tf_op jit(solution)/shard_map/ppermute | solution.py:17
  36.8 5.6 %collective-permute-start.1 = (f32[2,16,1]{2,1,0:T(8,128)S(1)}, f32[2,16,1]{2,1,0:T(8,128)S(1)}, u32[]{:S(2)}, u32[]{:S(2)}) collective-permute-start(f32[2,16,1]{2,1,0:T(8,128)S(1)} %get-tuple-element.14), channel_id=1, source_target_pairs={{1,0},{2,1},{3,2},{4,3},{5,4},{6,5},{7,6},{9,8},{10,9},{11,10},{12... | collective-permute-start | bytes 392 | tf_op jit(solution)/shard_map/ppermute | solution.py:19
  42.4 0.0 copy-done.3
  42.4 0.1 select_reduce_fusion
  42.5 0.2 fusion.17
  42.7 0.0 copy-done.2
  42.7 0.3 multiply_select_fusion
  43.1 1.1 copy.95
  44.2 0.0 collective-permute-done
  44.2 0.0 collective-permute-done.1
  44.2 0.8 concatenate.11
  45.0 2.4 collective-permute-start.2
  47.4 0.1 broadcast_add_fusion
  47.5 27.6 %collective-permute-done.2 = f32[2,16,8194]{2,1,0:T(8,128)S(1)} collective-permute-done((f32[2,16,8194]{2,1,0:T(8,128)S(1)}, f32[2,16,8194]{2,1,0:T(8,128)S(1)}, u32[]{:S(2)}, u32[]{:S(2)}) %collective-permute-start.2) | collective-permute-done | bytes 1048864 | tf_op jit(solution)/shard_map/ppermute | solution.py:33
  75.1 0.9 fusion.12
  76.0 7.9 %copy.79 = f32[2,16,8192]{1,0,2:T(2,128)} copy(f32[2,16,8192]{2,1,0:T(8,128)S(1)} %fusion.12) | data formatting | bytes 2097152 | tf_op jit(solution)/shard_map/add | solution.py:71
  83.9 103.3 %all-gather.2.cloned.1.call-done = f32[128,16,1024]{2,1,0:T(8,128)} async-done(((f32[2,16,1024]{2,1,0:T(8,128)}), f32[128,16,1024]{2,1,0:T(8,128)}) %all-gather.2.cloned.1.call-update) | async-done | bytes 8388624 | tf_op jit(solution)/shard_map/all_gather | solution.py:85
  187.2 17.9 %fusion = f32[128,16,1024]{2,0,1:T(8,128)S(1)} fusion(f32[128,16,1024]{2,1,0:T(8,128)} %all-gather.2.cloned.1.call-done, f32[128]{0:T(128)S(1)} %multiply_select_fusion.2, pred[128]{0:T(512)(128)(4,1)S(1)} %get-tuple-element.22, pred[128]{0:T(512)(128)(4,1)S(1)} %get-tuple-element.23), kind=kOutput, calls=%fused_computation.2 | convolution fusion | flops 3221307392 | bytes 16777984 | tf_op jit(solution)/shard_map/bk,kvr->bvr/dot_general | solution.py:82
  205.1 4.5 %fusion.8 = f32[1024,2,16]{0,1,2:T(2,128)S(1)} fusion(f32[128,16,1024]{2,0,1:T(8,128)S(1)} %fusion, f32[128,1024]{1,0:T(8,128)S(1)} %bitcast.28, f32[1024]{0:T(1024)S(1)} %get-tuple-element.20, f32[128,128]{0,1:T(8,128)S(1)} %multiply_select_fusion, s32[]{:T(128)S(6)} %select_n.115), kind=kOutput, calls=%fused_computation.8 | convolution fusion | flops 52461568 | bytes 9049092 | tf_op jit(solution)/shard_map/bk,bvr->kvr/dot_general | solution.py:90
  209.6 0.5 copy.80
  210.2 97.1 %scatter_fusion = f32[2,16,8192]{1,0,2:T(2,128)} fusion(f32[2,16,8192]{1,0,2:T(2,128)} %copy.79, s32[1024]{0:T(1024)S(1)} %get-tuple-element.17, f32[1024,2,16]{2,1,0:T(2,128)S(1)} %copy.80), kind=kCustom, calls=%fused_computation.1 | custom fusion | flops 32768 | bytes 397312 | tf_op jit(solution)/shard_map/scatter-add | solution.py:92
  307.3 9.3 %copy.85 = f32[2,16,8192]{2,1,0:T(8,128)S(1)} copy(f32[2,16,8192]{1,0,2:T(2,128)} %scatter_fusion) | data formatting | bytes 2097152
  316.6 0.0 copy-start.1
  316.6 1.5 convolution_bitcast_fusion
  318.1 1.4 convolution_bitcast_fusion.1
  319.6 109.0 %all-reduce = (f32[1,16,16]{1,2,0:T(8,128)S(1)}, f32[1,16,16]{1,2,0:T(8,128)S(1)}) all-reduce(f32[1,16,16]{1,2,0:T(8,128)S(1)} %convolution_bitcast_fusion, f32[1,16,16]{1,2,0:T(8,128)S(1)} %convolution_bitcast_fusion.1), channel_id=1, replica_groups=mesh['harm'=64,'grp'=8] {'harm','grp'}, use_global_device_ids=true, to_apply=%region_4.5 | all-reduce | flops 512 | bytes 4096 | tf_op jit(solution)/shard_map/psum | solution.py:95
  428.5 0.7 copy.86
  429.2 0.0 copy-done.1
  (7 shorter events, 0.1 us)
Async XLA Ops:
  7.2 25.0 %copy-start = (f32[2,16,8192]{2,1,0:T(8,128)S(1)}, f32[2,16,8192]{2,1,0:T(8,128)}, u32[]{:S(2)}) copy-start(f32[2,16,8192]{2,1,0:T(8,128)} %param.6) | copy-start | bytes 3145732
  7.2 35.2 %copy-start.3 = (s32[64]{0:T(128)S(1)}, s32[64]{0:T(128)}, u32[]{:S(2)}) copy-start(s32[64]{0:T(128)} %param.10) | copy-start | bytes 772
  7.2 35.5 %copy-start.2 = (f32[8192]{0:T(1024)S(1)}, f32[8192]{0:T(1024)}, u32[]{:S(2)}) copy-start(f32[8192]{0:T(1024)} %param.7) | copy-start | bytes 98308
  7.2 180.0 %all-gather.2.cloned.1.call-start = ((), (), s32[]{:S(2)}) async-start(), calls=%async_computation | async-start | bytes 8519680 | tf_op jit(solution)/shard_map/all_gather | solution.py:85
  32.2 12.0 %collective-permute-start = (f32[2,16,1]{2,1,0:T(8,128)S(1)}, f32[2,16,1]{2,1,0:T(8,128)S(1)}, u32[]{:S(2)}, u32[]{:S(2)}) collective-permute-start(f32[2,16,1]{2,1,0:T(8,128)S(1)} %get-tuple-element.15), channel_id=1, source_target_pairs={{0,1},{1,2},{2,3},{3,4},{4,5},{5,6},{6,7},{8,9},{9,10},{10,11},{11... | collective-permute-start | bytes 392 | tf_op jit(solution)/shard_map/ppermute | solution.py:17
  36.8 7.5 %collective-permute-start.1 = (f32[2,16,1]{2,1,0:T(8,128)S(1)}, f32[2,16,1]{2,1,0:T(8,128)S(1)}, u32[]{:S(2)}, u32[]{:S(2)}) collective-permute-start(f32[2,16,1]{2,1,0:T(8,128)S(1)} %get-tuple-element.14), channel_id=1, source_target_pairs={{1,0},{2,1},{3,2},{4,3},{5,4},{6,5},{7,6},{9,8},{10,9},{11,10},{12... | collective-permute-start | bytes 392 | tf_op jit(solution)/shard_map/ppermute | solution.py:19
  45.0 30.1 %collective-permute-start.2 = (f32[2,16,8194]{2,1,0:T(8,128)S(1)}, f32[2,16,8194]{2,1,0:T(8,128)S(1)}, u32[]{:S(2)}, u32[]{:S(2)}) collective-permute-start(f32[2,16,8194]{2,1,0:T(8,128)S(1)} %concatenate.11), channel_id=1, source_target_pairs={{0,256},{256,0},{8,264},{264,8},{16,272},{272,16},{24,280},{280,24... | collective-permute-start | bytes 3146504 | tf_op jit(solution)/shard_map/ppermute | solution.py:33
  316.6 112.6 %copy-start.1 = (f32[2,16,8192]{2,1,0:T(8,128)}, f32[2,16,8192]{2,1,0:T(8,128)S(1)}, u32[]{:S(2)}) copy-start(f32[2,16,8192]{2,1,0:T(8,128)S(1)} %copy.85) | copy-start | bytes 3145732
Sparse Core Ops, SparseCore 0:
  32.3 154.8 all-gather.1
where the time goes:
time: 438 us; the launch traced here: 436 us
  waiting for transfers between devices  131 us (30%)
  blocking collectives  109 us (25%)
  other arithmetic  105 us (24%)
  local copies, waits for them, and re-layouts  38.3 us (9%)
  matrix products  25.3 us (6%)
  between operations  14.9 us (3%)
  starting transfers between devices  12.5 us (3%)
    psum x1, blocking collectives, local(): first, second = lax.psum((first, second), ('harm', 'grp'))  109 us
    all_gather x1, waiting for transfers between devices, local(): lax.all_gather(rows, 'harm', axis=0, tiled=True)  103 us
    scatter-add x1, other arithmetic, local(): image = adjusted.at[:, :, attach].add(back)  97.1 us
    ppermute x1, waiting for transfers between devices, partner_2(): return lax.ppermute(block, axis, route)  27.6 us
    unnamed x12, local copies, waits for them, and re-layouts  21.1 us
    dot_general x1, matrix products, local(): jnp.einsum('bk,kvr->bvr', basis, lax.all_gather(rows, 'harm', axis=0, til...  17.9 us
  transfers between devices with their start and end apart: 4, of which 2 were waited for; matrix products, arithmetic and copies ran while one was open for 3% of the time, Pallas kernels for 0%

commit v1 on v0

v1 whole, which is shorter than its diff:
```python
import math

import jax
import jax.numpy as jnp
from jax import lax
from jax.experimental import pallas as pl
from jax.experimental.pallas import tpu as pltpu
from jax.sharding import PartitionSpec as P

LANES = 128
OCT = 8
PIECE = 16


def slot_tables(pair_harm, slots, blades):
    half = blades // 2
    onehot = (slots % half)[:, None] == jnp.arange(half, dtype=jnp.int32)[None, :]
    harmonic = jnp.sum(jnp.where(onehot, pair_harm[None, :], 0), axis=1)
    imag = slots >= half
    theta = jnp.where(
        harmonic == 0,
        jnp.where(imag, math.pi, 0.0),
        2.0 * math.pi * harmonic.astype(jnp.float32) / blades,
    )
    coup = jnp.where(harmonic == 0, 0.0, jnp.where(imag, -1.0, 1.0) * jnp.sin(theta))
    return (theta, coup, harmonic, imag)


def basis_table(theta, harmonic, imag, blades):
    blade_ids = jnp.arange(blades, dtype=jnp.float32)
    angle = blade_ids[:, None] * theta[None, :]
    wide = math.sqrt(2.0 / blades) * jnp.where(imag[None, :], jnp.sin(angle), jnp.cos(angle))
    return jnp.where(harmonic[None, :] == 0, jnp.cos(angle) / math.sqrt(blades), wide)


def iota(shape, dim):
    return lax.broadcasted_iota(jnp.int32, shape, dim)


def pick(tile, index):
    return jnp.take_along_axis(tile, index, axis=1, mode="promise_in_bounds")


def swap_blocks(tile):
    sub = iota(tile.shape, 0)
    block = iota(tile.shape, 1) // PIECE
    for bit in (1, 2, 4):
        from_low = pltpu.roll(pltpu.roll(tile, bit, 0), LANES - PIECE * bit, 1)
        from_high = pltpu.roll(pltpu.roll(tile, OCT - bit, 0), PIECE * bit, 1)
        s, b = (sub & bit) != 0, (block & bit) != 0
        tile = jnp.where(s & ~b, from_low, jnp.where(~s & b, from_high, tile))
    return tile


def gather_kernel(attach_ref, v_ref, out_ref):
    chunks, tiles = attach_ref.shape[0], v_ref.shape[2] // LANES
    low, high = [], []
    for c in range(chunks):
        col = jnp.broadcast_to(attach_ref[c : c + 1, :], (OCT, LANES))
        low.append(col & (LANES - 1))
        high.append(col >> 7)

    def step(i, accs):
        at = pl.ds(pl.multiple_of(i * LANES, LANES), LANES)
        tile = [v_ref[j // 2, OCT * (j % 2) : OCT * (j % 2) + OCT, at] for j in range(4)]
        new = []
        for c in range(chunks):
            here = high[c] == i
            for j in range(4):
                new.append(jnp.where(here, pick(tile[j], low[c]), accs[4 * c + j]))
        return tuple(new)

    zero = jnp.zeros((OCT, LANES), jnp.float32)
    accs = lax.fori_loop(0, tiles, step, (zero,) * (4 * chunks))
    for c in range(chunks):
        for j in range(4):
            out_ref[pl.ds(4 * OCT * c + j, OCT, stride=4), :] = swap_blocks(accs[4 * c + j])


def blade_kernel(where_ref, recv_ref, mistune_ref, basis_ref, basis_t_ref, out_ref):
    me, live = where_ref[0], where_ref[1]
    owners = recv_ref.shape[0] // 4
    part = [recv_ref[pl.ds(j, owners, stride=4), :] for j in range(4)]
    rows = jnp.concatenate(
        [jnp.concatenate([part[0], part[1]], axis=1), jnp.concatenate([part[2], part[3]], axis=1)], axis=0
    )
    blades = rows.shape[0]
    lane = iota((1, 2 * LANES), 1)
    alive = me * PIECE + (lane & (PIECE - 1)) < live
    rows = jnp.where(alive, rows, 0.0)
    blade = jnp.dot(basis_ref[...], rows, precision=lax.Precision.HIGHEST, preferred_element_type=jnp.float32)
    chunk = mistune_ref[pl.ds(me // OCT, blades, stride=OCT), :]
    index = (me % OCT) * PIECE + (iota((blades, LANES), 1) & (PIECE - 1))
    stiff = pick(chunk, index)
    forced = jnp.concatenate([stiff, stiff], axis=1) * blade
    back = jnp.dot(basis_t_ref[...], forced, precision=lax.Precision.HIGHEST, preferred_element_type=jnp.float32)
    back = jnp.where(alive, back, 0.0)
    for j in range(4):
        k2, vh = j // 2, j % 2
        out_ref[pl.ds(j, owners, stride=4), :] = back[owners * k2 : owners * (k2 + 1), LANES * vh : LANES * (vh + 1)]


def split3(x):
    a = x.astype(jnp.bfloat16)
    rest = x - a.astype(jnp.float32)
    b = rest.astype(jnp.bfloat16)
    return [a, b, (rest - b.astype(jnp.float32)).astype(jnp.bfloat16)]


def final_kernel(coef_ref, attach_ref, stiff_ref, v_ref, p_ref, recv_ref, image_ref, gram_ref, inv_ref, back_ref):
    tiles = stiff_ref.shape[0]
    rows = attach_ref.shape[1]
    chunks = rows // LANES
    attach = attach_ref[...]
    r = iota((1, rows), 1)
    in_tile = (iota((tiles, rows), 0) == (attach >> 7)).astype(jnp.bfloat16)
    in_lane = iota((LANES, rows), 0) == (attach & (LANES - 1))
    nt = (((1,), (1,)), ((), ()))
    for n, value in enumerate(((r >> 7) + 1, r & (LANES - 1))):
        weighted = jnp.where(in_lane, value.astype(jnp.float32), 0.0).astype(jnp.bfloat16)
        inv_ref[n] = lax.dot_general(in_tile, weighted, nt, preferred_element_type=jnp.float32).astype(jnp.int32)
    for c in range(chunks):
        for j in range(4):
            back_ref[4 * c + j] = swap_blocks(recv_ref[pl.ds(4 * OCT * c + j, OCT, stride=4), :])
    lane = iota((OCT, LANES), 1)
    first, last = lane == 0, lane == LANES - 1
    per = 4

    def step(g, total):
        gram = total
        wide = [[[], []], [[], []]]
        for t in range(per):
            i = g * per + t
            here = pl.ds(pl.multiple_of(i * LANES, LANES), LANES)
            after = pl.ds(pl.multiple_of((i + 1) * LANES, LANES), LANES)
            before = pl.ds(pl.multiple_of(jnp.where(i == 0, tiles, i - 1) * LANES, LANES), LANES)
            stiff = jnp.broadcast_to(stiff_ref[pl.ds(i, 1), :], (OCT, LANES))
            chunk = jnp.broadcast_to(inv_ref[0, pl.ds(i, 1), :], (OCT, LANES))
            index = jnp.broadcast_to(inv_ref[1, pl.ds(i, 1), :], (OCT, LANES))
            for j in range(4):
                k2, o = j // 2, OCT * (j % 2)
                v = v_ref[k2, o : o + OCT, here]
                lo = pltpu.roll(jnp.where(last, v_ref[k2, o : o + OCT, before], v), 1, 1)
                hi = pltpu.roll(jnp.where(first, v_ref[k2, o : o + OCT, after], v), LANES - 1, 1)
                p = p_ref[k2, o : o + OCT, here]
                plo = pltpu.roll(jnp.where(last, p_ref[k2, o : o + OCT, before], p), 1, 1)
                phi = pltpu.roll(jnp.where(first, p_ref[k2, o : o + OCT, after], p), LANES - 1, 1)
                value = (coef_ref[k2] + stiff) * v - lo - hi + coef_ref[2 + k2] * (phi - plo)
                back = jnp.zeros((OCT, LANES), jnp.float32)
                for c in range(chunks):
                    back = jnp.where(chunk == c + 1, pick(back_ref[4 * c + j], index), back)
                value = value + back
                image_ref[k2, o : o + OCT, here] = value
                wide[k2][j % 2].append((v, value))
        for k2 in range(2):
            v = jnp.concatenate([jnp.concatenate([x[0] for x in wide[k2][o]], axis=1) for o in range(2)], axis=0)
            w = jnp.concatenate([jnp.concatenate([x[1] for x in wide[k2][o]], axis=1) for o in range(2)], axis=0)
            left = jnp.concatenate(split3(v) + split3(w), axis=0)
            right = jnp.concatenate(split3(w), axis=0)
            gram = gram + lax.dot_general(left, right, nt, preferred_element_type=jnp.float32)
        return gram

    vecs = image_ref.shape[1]
    total = lax.fori_loop(0, tiles // per, step, jnp.zeros((6 * vecs, 3 * vecs), jnp.float32))
    for n in range(2):
        gram = jnp.zeros((vecs, vecs), jnp.float32)
        for a in range(3):
            for b in range(3 - a):
                at = (3 * n + a) * vecs
                gram = gram + total[at : at + vecs, b * vecs : (b + 1) * vecs]
        gram_ref[n] = gram


def vmem():
    return pl.BlockSpec(memory_space=pltpu.VMEM)


def smem():
    return pl.BlockSpec(memory_space=pltpu.SMEM)


def params():
    return pltpu.CompilerParams(vmem_limit_bytes=24 * 1024 * 1024)


def local(vectors, stiffness, attach, live, pair_harm, mistune):
    blades = pair_harm.shape[0] * 2
    slot_count, vecs, width = vectors.shape
    harm_size, grp_size = lax.axis_size("harm"), lax.axis_size("grp")
    me = lax.axis_index("harm")
    own_slots = me * slot_count + jnp.arange(slot_count, dtype=jnp.int32)
    theta, coup, _, _ = slot_tables(pair_harm, own_slots, blades)
    coef = jnp.concatenate([2.0 + 2.0 * (1.0 - jnp.cos(theta)), coup])

    ends = grp_size - 1
    low_edge = lax.ppermute(vectors[:, :, -1:], "grp", [(i, i + 1) for i in range(ends)])
    high_edge = lax.ppermute(vectors[:, :, :1], "grp", [(i + 1, i) for i in range(ends)])
    blank = jnp.zeros((slot_count, vecs, LANES - 2), jnp.float32)
    wide = jnp.concatenate([vectors, high_edge, blank, low_edge], axis=2)
    half = harm_size // 2
    partner = lax.ppermute(wide, "harm", [(i, i ^ half) for i in range(harm_size)])

    attach_tiles = attach.reshape(-1, LANES)
    packed = pl.pallas_call(
        gather_kernel,
        out_shape=jax.ShapeDtypeStruct((4 * harm_size, LANES), jnp.float32),
        in_specs=[vmem(), vmem()],
        out_specs=vmem(),
        compiler_params=params(),
        name="gather_rows",
    )(attach_tiles, vectors)
    recv = lax.all_to_all(packed.reshape(harm_size, 4, LANES), "harm", 0, 0)

    order = jnp.concatenate([jnp.arange(k, blades, slot_count, dtype=jnp.int32) for k in range(slot_count)])
    theta_all, _, harmonic_all, imag_all = slot_tables(pair_harm, order, blades)
    basis = basis_table(theta_all, harmonic_all, imag_all, blades)
    where = jnp.stack([me.astype(jnp.int32), live[0]])
    back = pl.pallas_call(
        blade_kernel,
        out_shape=jax.ShapeDtypeStruct((4 * harm_size, LANES), jnp.float32),
        in_specs=[smem(), vmem(), vmem(), vmem(), vmem()],
        out_specs=vmem(),
        compiler_params=params(),
        name="blades",
    )(where, recv.reshape(4 * harm_size, LANES), mistune.reshape(-1, LANES), basis, basis.T)
    back = lax.all_to_all(back.reshape(harm_size, 4, LANES), "harm", 0, 0)

    tiles = width // LANES
    image, gram = pl.pallas_call(
        final_kernel,
        out_shape=(
            jax.ShapeDtypeStruct(vectors.shape, jnp.float32),
            jax.ShapeDtypeStruct((2, vecs, vecs), jnp.float32),
        ),
        in_specs=[smem()] + [vmem()] * 5,
        out_specs=(vmem(), vmem()),
        scratch_shapes=[
            pltpu.VMEM((2, tiles, LANES), jnp.int32),
            pltpu.VMEM((4 * attach.shape[0] // LANES, OCT, LANES), jnp.float32),
        ],
        compiler_params=params(),
        name="image_gram",
    )(coef, attach.reshape(1, -1), stiffness.reshape(-1, LANES), wide, partner, back.reshape(4 * harm_size, LANES))

    part = gram.reshape(1, 4, LANES)
    part = lax.all_to_all(jnp.broadcast_to(part, (grp_size, 4, LANES)), "grp", 0, 0)
    part = jnp.sum(part, axis=0, keepdims=True)
    part = lax.all_to_all(jnp.broadcast_to(part, (harm_size, 4, LANES)), "harm", 0, 0)
    return (image, jnp.sum(part, axis=0).reshape(2, vecs, vecs))


def solution(mesh):
    in_specs = (P("harm", None, "grp"), P("grp"), P("grp"), P("grp"), P(), P(None, "grp", None))
    out_specs = (P("harm", None, "grp"), P())
    return jax.shard_map(local, mesh=mesh, in_specs=in_specs, out_specs=out_specs, check_vma=False)
```

time: 438 us -> 119 us (0.27)
  waiting for transfers between devices: 131 us -> 22.7 us
  other arithmetic: 105 us -> 1.34 us
  blocking collectives: 109 us -> 31 us
  local copies, waits for them, and re-layouts: 38.3 us -> 4.83 us
  matrix products: 25.3 us -> 0 us
  starting transfers between devices: 12.5 us -> 35.2 us
  Pallas kernels: 0 us -> 20.8 us
  between operations: 14.9 us -> 1.43 us
    psum x1 -> x0, blocking collectives: 109 us -> none  [local(): first, second = lax.psum((first, second), ('harm', 'grp'))]
    all_gather x1 -> x0, waiting for transfers between devices: 103 us -> none  [local(): lax.all_gather(rows, 'harm', axis=0, tiled=True)]
    scatter-add x1 -> x0, other arithmetic: 97.1 us -> none  [local(): image = adjusted.at[:, :, attach].add(back)]
    all_to_all x0 -> x2, blocking collectives: none -> 31 us  [the longest x1 19 us: local(): lax.all_to_all(jnp.broadcast_to(part, (harm_size, 4, LANES)), 'harm', 0, 0)]
    ppermute x3, waiting for transfers between devices: 27.6 us -> 0.01 us  [the longest x1 0.01 us: local(): lax.ppermute(vectors[:, :, -1:], 'grp', [(i, i + 1) for i in range(ends)])]
    dot_general x4 -> x0, matrix products: 25.3 us -> none  [the longest x1 17.9 us: local(): jnp.einsum('bk,kvr->bvr', basis, lax.all_gather(rows, 'harm', axis=0, til...]
    all_to_all x0 -> x2, waiting for transfers between devices: none -> 22.7 us  [the longest x1 14.2 us: local(): back = lax.all_to_all(back.reshape(harm_size, 4, LANES), 'harm', 0, 0)]
    pallas_call x0 -> x3, Pallas kernels: none -> 20.8 us  [the longest x1 9.72 us: local(): pl.pallas_call(final_kernel, out_shape=(jax.ShapeDtypeStruct(vectors.shap...]
  transfers between devices with their start and end apart: 4 -> 5, of which waited for: 2 -> 2; matrix products, arithmetic and copies ran while one was open for 3% -> 1% of each run, Pallas kernels for 0% -> 9%
where the time goes in v1:
time: 119 us; the launch traced here: 117 us
  starting transfers between devices  35.2 us (30%)
  blocking collectives  31 us (26%)
  waiting for transfers between devices  22.7 us (19%)
  Pallas kernels  20.8 us (17%)
  local copies, waits for them, and re-layouts  4.83 us (4%)
  between operations  1.43 us (1%)
  other arithmetic  1.34 us (1%)
    all_to_all x1, blocking collectives, local(): lax.all_to_all(jnp.broadcast_to(part, (harm_size, 4, LANES)), 'harm', 0, 0)  19 us
    all_to_all x1, starting transfers between devices, local(): recv = lax.all_to_all(packed.reshape(harm_size, 4, LANES), 'harm', 0, 0)  14.8 us
    all_to_all x1, waiting for transfers between devices, local(): back = lax.all_to_all(back.reshape(harm_size, 4, LANES), 'harm', 0, 0)  14.2 us
    all_to_all x1, blocking collectives, local(): lax.all_to_all(jnp.broadcast_to(part, (grp_size, 4, LANES)), 'grp', 0, 0)  11.9 us
    pallas_call x1, Pallas kernels, local(): pl.pallas_call(final_kernel, out_shape=(jax.ShapeDtypeStruct(vectors.shap...  9.72 us
    pallas_call x1, Pallas kernels, local(): pl.pallas_call(gather_kernel, out_shape=jax.ShapeDtypeStruct((4 * harm_si...  9.19 us
    all_to_all x1, waiting for transfers between devices, local(): recv = lax.all_to_all(packed.reshape(harm_size, 4, LANES), 'harm', 0, 0)  8.46 us
    all_to_all x1, starting transfers between devices, local(): back = lax.all_to_all(back.reshape(harm_size, 4, LANES), 'harm', 0, 0)  5.71 us
  transfers between devices with their start and end apart: 5, of which 2 were waited for; matrix products, arithmetic and copies ran while one was open for 1% of the time, Pallas kernels for 9%

profile of v1, /device:TPU:1, one launch (start us, length us, event | category | flops | bytes accessed | tf_op | source)
XLA Modules:
  0.0 117.3 jit_solution(1727460736019225852)
XLA Ops:
  0.6 0.0 copy-start.6
  0.6 0.8 fusion.4
  1.5 4.5 %collective-permute-start.1 = (f32[2,16,1]{2,1,0:T(8,128)S(1)}, f32[2,16,1]{2,1,0:T(8,128)S(1)}, u32[]{:S(2)}, u32[]{:S(2)}) collective-permute-start(f32[2,16,1]{2,1,0:T(8,128)S(1)} %get-tuple-element.8), channel_id=1, source_target_pairs={{0,1},{1,2},{2,3},{3,4},{4,5},{5,6},{6,7},{8,9},{9,10},{10,11},{11... | collective-permute-start | bytes 392 | tf_op jit(solution)/shard_map/ppermute | solution.py:196
  6.0 5.6 %collective-permute-start = (f32[2,16,1]{2,1,0:T(8,128)S(1)}, f32[2,16,1]{2,1,0:T(8,128)S(1)}, u32[]{:S(2)}, u32[]{:S(2)}) collective-permute-start(f32[2,16,1]{2,1,0:T(8,128)S(1)} %get-tuple-element.9), channel_id=1, source_target_pairs={{1,0},{2,1},{3,2},{4,3},{5,4},{6,5},{7,6},{9,8},{10,9},{11,10},{12... | collective-permute-start | bytes 392 | tf_op jit(solution)/shard_map/ppermute | solution.py:197
  11.5 0.0 copy-start
  11.5 1.2 %copy-done = f32[2,16,8192]{2,1,0:T(8,128)S(1)} copy-done((f32[2,16,8192]{2,1,0:T(8,128)S(1)}, f32[2,16,8192]{2,1,0:T(8,128)}, u32[]{:S(2)}) %copy-start) | copy-done | bytes 1048600
  12.8 0.0 copy-start.4
  12.8 0.7 copy-done.4
  13.5 0.0 copy-start.1
  13.5 9.2 %gather_rows.1 = f32[256,128]{1,0:T(8,128)} custom-call(s32[8,128]{1,0:T(8,128)S(1)} %bitcast.13, f32[2,16,8192]{2,1,0:T(8,128)S(1)} %copy-done), custom_call_target="tpu_custom_call" | custom-call | tf_op jit(solution)/shard_map/gather_rows/pallas_call | solution.py:204
  22.6 14.8 %all-to-all-start = ((f32[64,4,128]{2,1,0:T(4,128)}), f32[64,4,128]{2,1,0:T(4,128)S(1)}, u32[]{:S(2)}, u32[]{:S(2)}) async-start(f32[64,4,128]{2,1,0:T(4,128)} %bitcast.4), calls=%async_computation | async-start | bytes 262144 | tf_op jit(solution)/shard_map/all_to_all | solution.py:212
  37.5 0.1 and_select_fusion
  37.6 0.0 copy-done.6
  37.6 0.1 select_reduce_fusion
  38.3 0.0 collective-permute-done.1
  38.3 0.0 collective-permute-done
  38.4 0.0 copy-done.1
  38.4 0.2 concatenate.27.v_ref
  38.6 0.0 copy-start.3
  38.6 0.0 copy-start.5
  38.6 4.7 %collective-permute-start.2 = (f32[2,16,8320]{2,1,0:T(8,128)S(1)}, f32[2,16,8320]{2,1,0:T(8,128)S(1)}, u32[]{:S(2)}, u32[]{:S(2)}) collective-permute-start(f32[2,16,8320]{2,1,0:T(8,128)S(1)} %concatenate.27.v_ref), channel_id=1, source_target_pairs={{0,256},{8,264},{16,272},{24,280},{32,288},{40,296},{48,304},{56,3... | collective-permute-start | bytes 3194888 | tf_op jit(solution)/shard_map/ppermute | solution.py:201
  43.3 0.1 pad_add_fusion.where_ref
  43.4 0.1 multiply_select_fusion.2
  43.4 0.6 multiply_select_fusion
  44.0 8.5 %all-to-all-done = f32[64,4,128]{2,1,0:T(4,128)S(1)} async-done(((f32[64,4,128]{2,1,0:T(4,128)}), f32[64,4,128]{2,1,0:T(4,128)S(1)}, u32[]{:S(2)}, u32[]{:S(2)}) %all-to-all-start) | async-done | bytes 131104 | tf_op jit(solution)/shard_map/all_to_all | solution.py:212
  52.5 0.0 copy-start.2
  52.5 1.0 copy-done.2
  53.5 1.9 %blades.1 = f32[256,128]{1,0:T(8,128)} custom-call(s32[2]{0:T(128)S(1)} %pad_add_fusion.where_ref, f32[256,128]{1,0:T(8,128)S(1)} %bitcast.9, f32[1024,128]{1,0:T(8,128)S(1)} %bitcast.11, f32[128,128]{1,0:T(8,128)S(1)} %get-tuple-element.11.basis_ref, f32[128,128]{1,0:T(8,128)S(1)} %get-tuple-element.10.basis_t_ref), custom_call_target="tpu_custom_call" | custom-call | tf_op jit(solution)/shard_map/blades/pallas_call | solution.py:218
  55.4 5.7 %all-to-all-start.1 = ((f32[64,4,128]{2,1,0:T(4,128)}), f32[64,4,128]{2,1,0:T(4,128)S(1)}, u32[]{:S(2)}, u32[]{:S(2)}) async-start(f32[64,4,128]{2,1,0:T(4,128)} %bitcast.7), calls=%async_computation.1 | async-start | bytes 262144 | tf_op jit(solution)/shard_map/all_to_all | solution.py:226
  61.1 0.2 fusion
  61.4 0.1 pad_maximum_fusion.coef_ref
  61.4 14.2 %all-to-all-done.1 = f32[64,4,128]{2,1,0:T(4,128)S(1)} async-done(((f32[64,4,128]{2,1,0:T(4,128)}), f32[64,4,128]{2,1,0:T(4,128)S(1)}, u32[]{:S(2)}, u32[]{:S(2)}) %all-to-all-start.1) | async-done | bytes 131104 | tf_op jit(solution)/shard_map/all_to_all | solution.py:226
  75.7 0.0 collective-permute-done.2.p_ref
  75.7 0.0 copy-done.3
  75.7 0.0 copy-done.5
  75.7 9.7 %image_gram.1 = (f32[2,16,8192]{2,1,0:T(8,128)}, f32[2,16,16]{2,1,0:T(8,128)S(1)}) custom-call(f32[4]{0:T(128)S(1)} %pad_maximum_fusion.coef_ref, s32[1,1024]{1,0:T(1,128)S(1)} %bitcast.14, f32[64,128]{1,0:T(8,128)S(1)} %bitcast.12, f32[2,16,8320]{2,1,0:T(8,128)S(1)} %concatenate.27.v_ref, f32[2,16,8320]{2,1,0:T(8,128)S(1)} %collective-permute-done.2.p_ref, ...), custom_call_target="tpu_custom_call" | custom-call | tf_op jit(solution)/shard_map/image_gram/pallas_call | solution.py:229
  85.4 0.1 broadcast_in_dim.103
  85.5 11.9 %all_to_all.20 = f32[8,4,128]{2,1,0:T(4,128)S(1)} all-to-all(f32[8,4,128]{2,1,0:T(4,128)S(1)} %broadcast_in_dim.104), channel_id=1, replica_groups=mesh['harm'=64,'grp'=8] {'grp'}, dimensions={0} | all-to-all | bytes 32768 | tf_op jit(solution)/shard_map/all_to_all | solution.py:246
  97.5 19.0 %all_to_all.21 = f32[64,4,128]{2,1,0:T(4,128)S(1)} all-to-all(f32[64,4,128]{2,1,0:T(4,128)S(1)} %broadcast_in_dim.105), channel_id=1, replica_groups=mesh['harm'=64,'grp'=8] {'harm'}, dimensions={0} | all-to-all | bytes 262144 | tf_op jit(solution)/shard_map/all_to_all | solution.py:248
  116.5 0.1 reduce_sum.39
  116.6 0.7 reshape.128
  (8 shorter events, 0.1 us)
Async XLA Ops:
  0.6 36.9 %copy-start.6 = (s32[64]{0:T(128)S(1)}, s32[64]{0:T(128)}, u32[]{:S(2)}) copy-start(s32[64]{0:T(128)} %param.10) | copy-start | bytes 772
  1.5 36.9 %collective-permute-start.1 = (f32[2,16,1]{2,1,0:T(8,128)S(1)}, f32[2,16,1]{2,1,0:T(8,128)S(1)}, u32[]{:S(2)}, u32[]{:S(2)}) collective-permute-start(f32[2,16,1]{2,1,0:T(8,128)S(1)} %get-tuple-element.8), channel_id=1, source_target_pairs={{0,1},{1,2},{2,3},{3,4},{4,5},{5,6},{6,7},{8,9},{9,10},{10,11},{11... | collective-permute-start | bytes 392 | tf_op jit(solution)/shard_map/ppermute | solution.py:196
  6.0 32.4 %collective-permute-start = (f32[2,16,1]{2,1,0:T(8,128)S(1)}, f32[2,16,1]{2,1,0:T(8,128)S(1)}, u32[]{:S(2)}, u32[]{:S(2)}) collective-permute-start(f32[2,16,1]{2,1,0:T(8,128)S(1)} %get-tuple-element.9), channel_id=1, source_target_pairs={{1,0},{2,1},{3,2},{4,3},{5,4},{6,5},{7,6},{9,8},{10,9},{11,10},{12... | collective-permute-start | bytes 392 | tf_op jit(solution)/shard_map/ppermute | solution.py:197
  11.5 1.2 %copy-start = (f32[2,16,8192]{2,1,0:T(8,128)S(1)}, f32[2,16,8192]{2,1,0:T(8,128)}, u32[]{:S(2)}) copy-start(f32[2,16,8192]{2,1,0:T(8,128)} %v_ref.1) | copy-start | bytes 3145732
  12.8 0.7 copy-start.4
  13.5 24.9 %copy-start.1 = (f32[2,16,8192]{2,1,0:T(8,128)S(1)}, f32[2,16,8192]{2,1,0:T(8,128)}, u32[]{:S(2)}) copy-start(f32[2,16,8192]{2,1,0:T(8,128)} %v_ref.1) | copy-start | bytes 3145732
  22.6 29.8 %all-to-all-start = ((f32[64,4,128]{2,1,0:T(4,128)}), f32[64,4,128]{2,1,0:T(4,128)S(1)}, u32[]{:S(2)}, u32[]{:S(2)}) async-start(f32[64,4,128]{2,1,0:T(4,128)} %bitcast.4), calls=%async_computation | async-start | bytes 262144 | tf_op jit(solution)/shard_map/all_to_all | solution.py:212
  38.6 37.1 %copy-start.3 = (f32[8192]{0:T(1024)S(1)}, f32[8192]{0:T(1024)}, u32[]{:S(2)}) copy-start(f32[8192]{0:T(1024)} %param.7) | copy-start | bytes 98308
  38.6 37.1 %copy-start.5 = (s32[1024]{0:T(1024)S(1)}, s32[1024]{0:T(1024)}, u32[]{:S(2)}) copy-start(s32[1024]{0:T(1024)} %param.8) | copy-start | bytes 12292
  38.6 37.1 %collective-permute-start.2 = (f32[2,16,8320]{2,1,0:T(8,128)S(1)}, f32[2,16,8320]{2,1,0:T(8,128)S(1)}, u32[]{:S(2)}, u32[]{:S(2)}) collective-permute-start(f32[2,16,8320]{2,1,0:T(8,128)S(1)} %concatenate.27.v_ref), channel_id=1, source_target_pairs={{0,256},{8,264},{16,272},{24,280},{32,288},{40,296},{48,304},{56,3... | collective-permute-start | bytes 3194888 | tf_op jit(solution)/shard_map/ppermute | solution.py:201
  52.5 1.0 copy-start.2
  55.4 20.3 %all-to-all-start.1 = ((f32[64,4,128]{2,1,0:T(4,128)}), f32[64,4,128]{2,1,0:T(4,128)S(1)}, u32[]{:S(2)}, u32[]{:S(2)}) async-start(f32[64,4,128]{2,1,0:T(4,128)} %bitcast.7), calls=%async_computation.1 | async-start | bytes 262144 | tf_op jit(solution)/shard_map/all_to_all | solution.py:226

commit v2 on v0

v2 whole, which is shorter than its diff:
```python
import math

import jax
import jax.numpy as jnp
from jax import lax
from jax.experimental import pallas as pl
from jax.experimental.pallas import tpu as pltpu
from jax.sharding import PartitionSpec as P

LANES = 128
OCT = 8
PIECE = 16


def iota(shape, dim):
    return lax.broadcasted_iota(jnp.int32, shape, dim)


def pick(tile, index):
    return jnp.take_along_axis(tile, index, axis=1, mode="promise_in_bounds")


def swap_blocks(tile):
    sub = iota(tile.shape, 0)
    block = iota(tile.shape, 1) // PIECE
    for bit in (1, 2, 4):
        from_low = pltpu.roll(pltpu.roll(tile, bit, 0), LANES - PIECE * bit, 1)
        from_high = pltpu.roll(pltpu.roll(tile, OCT - bit, 0), PIECE * bit, 1)
        s, b = (sub & bit) != 0, (block & bit) != 0
        tile = jnp.where(s & ~b, from_low, jnp.where(~s & b, from_high, tile))
    return tile


NT = (((1,), (1,)), ((), ()))
TN = (((0,), (0,)), ((), ()))


def dot_f32(a, b, dims):
    return lax.dot_general(a, b, dims, precision=lax.Precision.HIGHEST, preferred_element_type=jnp.float32)


def split(x, parts):
    out = []
    for _ in range(parts):
        out.append(x.astype(jnp.bfloat16))
        x = x - out[-1].astype(jnp.float32)
    return out


def angle_of(harmonic, imag, slots):
    wide = 2.0 * math.pi * harmonic.astype(jnp.float32) / slots
    return jnp.where(harmonic == 0, jnp.where(imag, math.pi, 0.0), wide)


def harm_index():
    return lax.axis_index("y") * lax.axis_size("z") + lax.axis_index("z")


def own_terms(pair_ref, k2):
    half = pair_ref.shape[0]
    slot = 2 * harm_index() + k2
    harmonic = jnp.full((OCT, LANES), pair_ref[lax.rem(slot, half)], jnp.int32)
    imag = jnp.full((OCT, LANES), slot, jnp.int32) >= half
    theta = angle_of(harmonic, imag, 2 * half)
    coup = jnp.where(harmonic == 0, 0.0, jnp.where(imag, -1.0, 1.0) * jnp.sin(theta))
    return 2.0 + 2.0 * (1.0 - jnp.cos(theta)), coup


OCTETS = [(j // 2, slice(OCT * (j % 2), OCT * (j % 2) + OCT)) for j in range(4)]


def fetch(attach_ref, t_ref, g_ref):
    group = 16

    def step(n, carry):
        for u in range(group):
            at = attach_ref[n * group + u]
            g_ref[pl.ds(pl.multiple_of(n * group, group) + u, 1), :] = t_ref[pl.ds(at, 1), :]
        return carry

    lax.fori_loop(0, attach_ref.shape[0] // group, step, 0)


def gather_kernel(attach_ref, v_ref, out_ref, t_ref, g_ref):
    def step(i, carry):
        here = pl.ds(pl.multiple_of(i * LANES, LANES), LANES)
        t_ref[here, :] = jnp.concatenate([v_ref[k2, o, here] for k2, o in OCTETS], axis=0).T
        return carry

    lax.fori_loop(0, v_ref.shape[2] // LANES, step, 0, unroll=8)
    fetch(attach_ref, t_ref, g_ref)
    owners = out_ref.shape[0] // 4
    part = iota((owners, LANES), 1) // 32
    for m in range(4):
        out = None
        for b in range(4):
            x = jnp.concatenate([g_ref[pl.ds(4 * b + m, owners, stride=PIECE), :]] * 4, axis=1)
            out = x if out is None else jnp.where(part == b, x, out)
        out_ref[pl.ds(m, owners, stride=4), :] = out


def table_kernel(pair_ref, attach_ref, partner_ref, basis_ref, inv_ref):
    tiles, rows = inv_ref.shape[1], attach_ref.shape[1]
    attach = attach_ref[...]
    r = iota((1, rows), 1)
    in_tile = (iota((tiles, rows), 0) == (attach >> 7)).astype(jnp.float32).astype(jnp.bfloat16)
    in_lane = iota((LANES, rows), 0) == (attach & (LANES - 1))
    for n, value in enumerate(((r >> 7) + 1, r & (LANES - 1))):
        weighted = jnp.where(in_lane, value.astype(jnp.float32), 0.0).astype(jnp.bfloat16)
        inv_ref[n] = lax.dot_general(in_tile, weighted, NT, preferred_element_type=jnp.float32).astype(jnp.int32)

    half = pair_ref.shape[1]
    slots = 2 * half
    pairs = jnp.broadcast_to(jnp.concatenate([pair_ref[...]] * 2, axis=1), (OCT, slots))
    lane = iota((OCT, slots), 1)
    slot = 2 * (lane & (half - 1)) + lane // half
    harmonic = pick(pairs, slot & (half - 1))
    imag = slot >= half
    theta = angle_of(harmonic, imag, slots)
    for n in range(slots // OCT):
        angle = (iota((OCT, slots), 0) + OCT * n).astype(jnp.float32) * theta
        cosine = jnp.cos(angle)
        wide = math.sqrt(2.0 / slots) * jnp.where(imag, jnp.sin(angle), cosine)
        basis_ref[OCT * n : OCT * (n + 1), :] = jnp.where(harmonic == 0, cosine / math.sqrt(slots), wide)


def shifted(ref, k2, o, i, count, low, high):
    here = pl.ds(pl.multiple_of(i * LANES, LANES), LANES)
    after = pl.ds(pl.multiple_of(jnp.minimum(i + 1, count - 1) * LANES, LANES), LANES)
    before = pl.ds(pl.multiple_of(jnp.maximum(i - 1, 0) * LANES, LANES), LANES)
    lane = iota((OCT, LANES), 1)
    v = ref[k2, o, here]
    prev = jnp.where(i == 0, low, ref[k2, o, before])
    follow = jnp.where(i == count - 1, high, ref[k2, o, after])
    lo = pltpu.roll(jnp.where(lane == LANES - 1, prev, v), 1, 1)
    hi = pltpu.roll(jnp.where(lane == 0, follow, v), LANES - 1, 1)
    return v, lo, hi


def adjust_kernel(pair_ref, attach_ref, stiff_ref, v_ref, p_ref, low_ref, high_ref, p_edge_ref, adj_ref, gram_ref, cols_ref, t_ref, g_ref):
    tiles, vecs, per = stiff_ref.shape[0], v_ref.shape[1], 4
    terms = [own_terms(pair_ref, k2) for k2 in range(2)]

    def edge(ref, k2, o, n):
        return jnp.broadcast_to(ref[k2, o, n : n + 1], (OCT, LANES))

    low = [edge(low_ref, k2, o, 0) for k2, o in OCTETS]
    high = [edge(high_ref, k2, o, 0) for k2, o in OCTETS]
    p_low = [edge(p_edge_ref, k2, o, 0) for k2, o in OCTETS]
    p_high = [edge(p_edge_ref, k2, o, 1) for k2, o in OCTETS]

    def step(g, gram):
        vs, ws = [], []
        for t in range(per):
            i = g * per + t
            here = pl.ds(pl.multiple_of(i * LANES, LANES), LANES)
            stiff = jnp.broadcast_to(stiff_ref[pl.ds(i, 1), :], (OCT, LANES))
            v_tile, w_tile = [], []
            for j, (k2, o) in enumerate(OCTETS):
                v, lo, hi = shifted(v_ref, k2, o, i, tiles, low[j], high[j])
                _, p_lo, p_hi = shifted(p_ref, k2, o, i, tiles, p_low[j], p_high[j])
                w = (terms[k2][0] + stiff) * v - lo - hi + terms[k2][1] * (p_hi - p_lo)
                adj_ref[k2, o, here] = w
                v_tile.append(v)
                w_tile.append(w)
            t_ref[here, :] = jnp.concatenate(v_tile + w_tile, axis=0).T
            vs.append(jnp.concatenate(v_tile, axis=0))
            ws.append(jnp.concatenate(w_tile, axis=0))
        v, w = jnp.concatenate(vs, axis=1), jnp.concatenate(ws, axis=1)
        for k2 in range(2):
            own = slice(vecs * k2, vecs * (k2 + 1))
            w3 = split(w[own], 3)
            left = jnp.concatenate(split(v[own], 3) + w3, axis=0)
            gram = gram + lax.dot_general(left, jnp.concatenate(w3, axis=0), NT, preferred_element_type=jnp.float32)
        return gram

    total = lax.fori_loop(0, tiles // per, step, jnp.zeros((6 * vecs, 3 * vecs), jnp.float32), unroll=2)
    for n in range(2):
        gram = jnp.zeros((vecs, vecs), jnp.float32)
        for a in range(3):
            for b in range(3 - a):
                at = (3 * n + a) * vecs
                gram = gram + total[at : at + vecs, b * vecs : (b + 1) * vecs]
        gram_ref[n * vecs : (n + 1) * vecs, :] = gram
    fetch(attach_ref, t_ref, g_ref)
    for c in range(cols_ref.shape[1] // LANES):
        here = slice(LANES * c, LANES * (c + 1))
        cols_ref[:, here] = g_ref[here, :].T


def blade_kernel(live_ref, recv_ref, mistune_ref, basis_ref, out_ref):
    me, live = harm_index(), live_ref[0]
    owners = out_ref.shape[0] // 4
    blades = 2 * owners
    slab = [recv_ref[pl.ds(m, owners, stride=4), :] for m in range(4)]
    piece = iota((owners, LANES), 1) // PIECE

    def arrived(k2):
        halves = []
        for half in range(2):
            out = None
            for n in range(OCT):
                r = OCT * half + n
                at = 2 * (r // 4) + k2
                tile = slab[r % 4] if at == n else pltpu.roll(slab[r % 4], (PIECE * (n - at)) % LANES, 1)
                out = tile if out is None else jnp.where(piece == n, tile, out)
            halves.append(out)
        return jnp.concatenate(halves, axis=1)

    wide = 2 * LANES
    alive = me * PIECE + iota((1, wide), 1) // PIECE < live
    rows = jnp.where(alive, jnp.concatenate([arrived(0), arrived(1)], axis=0), 0.0)
    mm = (((1,), (0,)), ((), ()))
    blade = dot_f32(basis_ref[...], rows, mm)
    chunk = mistune_ref[pl.ds(me // OCT, blades, stride=OCT), :]
    index = lax.rem(me, OCT) * PIECE + iota((blades, LANES), 1) // PIECE
    stiff = jnp.concatenate([pick(chunk, index), pick(chunk, index + OCT)], axis=1)
    back = jnp.where(alive, dot_f32(basis_ref[...], stiff * blade, TN), 0.0)
    down, across = iota((wide, wide), 0), iota((wide, wide), 1)
    swap = ((down & (PIECE - 1)) == across // PIECE) & (down // PIECE == (across & (PIECE - 1)))
    turned = dot_f32(back, swap.astype(jnp.float32), mm)
    for j in range(4):
        k2, vh = j // 2, j % 2
        out_ref[pl.ds(j, owners, stride=4), :] = turned[owners * k2 : owners * (k2 + 1), LANES * vh : LANES * (vh + 1)]


def cross_kernel(recv_ref, cols_ref, gram_ref, total_ref, back_ref):
    vecs, chunks = gram_ref.shape[1], cols_ref.shape[1] // LANES
    tiles = [[swap_blocks(recv_ref[pl.ds(4 * OCT * c + j, OCT, stride=4), :]) for c in range(chunks)] for j in range(4)]
    total = gram_ref[...]
    for k2 in range(2):
        both = []
        for j in (2 * k2, 2 * k2 + 1):
            for c in range(chunks):
                back_ref[4 * c + j] = tiles[j][c]
            both.append(jnp.concatenate(tiles[j], axis=1))
        back = jnp.concatenate(both, axis=0)
        left = jnp.concatenate(
            [cols_ref[vecs * k2 : vecs * (k2 + 1), :], cols_ref[vecs * (k2 + 2) : vecs * (k2 + 3), :] + 0.5 * back], axis=0
        )
        term = dot_f32(left, back, NT)
        twice = dot_f32(back, left[vecs:], NT)
        total = total + term + jnp.concatenate([jnp.zeros_like(twice), twice], axis=0)
    total_ref[...] = total


def image_kernel(inv_ref, adj_ref, back_ref, image_ref):
    tiles, chunks = inv_ref.shape[1], back_ref.shape[0] // 4

    def step(i, carry):
        here = pl.ds(pl.multiple_of(i * LANES, LANES), LANES)
        chunk = jnp.broadcast_to(inv_ref[0, pl.ds(i, 1), :], (OCT, LANES))
        index = jnp.broadcast_to(inv_ref[1, pl.ds(i, 1), :], (OCT, LANES))
        for j, (k2, o) in enumerate(OCTETS):
            back = jnp.zeros((OCT, LANES), jnp.float32)
            for c in range(chunks):
                back = jnp.where(chunk == c + 1, pick(back_ref[4 * c + j], index), back)
            image_ref[k2, o, here] = adj_ref[k2, o, here] + back
        return carry

    lax.fori_loop(0, tiles, step, 0, unroll=8)


def vmem():
    return pl.BlockSpec(memory_space=pltpu.VMEM)


def smem():
    return pl.BlockSpec(memory_space=pltpu.SMEM)


def params(mebibytes):
    return pltpu.CompilerParams(vmem_limit_bytes=mebibytes * 1024 * 1024)


def cost(microseconds):
    return pl.CostEstimate(flops=int(microseconds * 1e9), bytes_accessed=0, transcendentals=0)


HARM, GRP, PLANE = ("y", "z"), ("x", "core"), ("y", "x", "core")


def spread_sum(part, axes):
    count = math.prod(lax.axis_size(axis) for axis in axes)
    return jnp.sum(lax.all_to_all(jnp.broadcast_to(part[None], (count,) + part.shape), axes, 0, 0), axis=0)


def local(vectors, stiffness, attach, live, pair_harm, mistune):
    slot_count, vecs, width = vectors.shape
    rows, blades, tiles = attach.shape[0], 2 * pair_harm.shape[0], width // LANES
    harm_size = lax.axis_size("y") * lax.axis_size("z")
    grp_size = lax.axis_size("x") * lax.axis_size("core")
    block = jax.ShapeDtypeStruct(vectors.shape, jnp.float32)
    packed_rows = jax.ShapeDtypeStruct((4 * harm_size, LANES), jnp.float32)

    half = harm_size // 2
    to_partner = [(i, i ^ half) for i in range(harm_size)]
    partner = lax.ppermute(vectors, HARM, to_partner)
    ends = grp_size - 1
    low_edge = lax.ppermute(vectors[:, :, -1:], GRP, [(i, i + 1) for i in range(ends)])
    high_edge = lax.ppermute(vectors[:, :, :1], GRP, [(i + 1, i) for i in range(ends)])
    partner_edge = lax.ppermute(jnp.concatenate([low_edge, high_edge], axis=2), HARM, to_partner)

    packed = pl.pallas_call(
        gather_kernel,
        out_shape=packed_rows,
        in_specs=[smem(), vmem()],
        out_specs=vmem(),
        scratch_shapes=[pltpu.VMEM((width, 2 * vecs), jnp.float32), pltpu.VMEM((rows, 2 * vecs), jnp.float32)],
        compiler_params=params(16),
        cost_estimate=cost(5),
        name="gather",
    )(attach, vectors)
    recv = lax.all_to_all(packed.reshape(harm_size, 4, LANES), HARM, 0, 0)

    basis, inv = pl.pallas_call(
        table_kernel,
        out_shape=(
            jax.ShapeDtypeStruct((blades, blades), jnp.float32),
            jax.ShapeDtypeStruct((2, tiles, LANES), jnp.int32),
        ),
        in_specs=[vmem()] * 2 + [pl.BlockSpec(memory_space=pl.ANY)],
        out_specs=(vmem(),) * 2,
        compiler_params=params(8),
        cost_estimate=cost(60),
        name="tables",
    )(pair_harm.reshape(1, -1), attach.reshape(1, -1), partner)
    back = pl.pallas_call(
        blade_kernel,
        out_shape=packed_rows,
        in_specs=[smem()] + [vmem()] * 3,
        out_specs=vmem(),
        compiler_params=params(16),
        cost_estimate=cost(4),
        name="blades",
    )(live, recv.reshape(4 * harm_size, LANES), mistune.reshape(-1, LANES), basis)
    back = lax.all_to_all(back.reshape(harm_size, 4, LANES), HARM, 0, 0)

    adj, gram, cols = pl.pallas_call(
        adjust_kernel,
        out_shape=(
            block,
            jax.ShapeDtypeStruct((2 * vecs, vecs), jnp.float32),
            jax.ShapeDtypeStruct((4 * vecs, rows), jnp.float32),
        ),
        in_specs=[smem(), smem()] + [vmem()] * 6,
        out_specs=(vmem(),) * 3,
        scratch_shapes=[pltpu.VMEM((width, 4 * vecs), jnp.float32), pltpu.VMEM((rows, 4 * vecs), jnp.float32)],
        compiler_params=params(16),
        cost_estimate=cost(40),
        name="adjust",
    )(pair_harm, attach, stiffness.reshape(-1, LANES), vectors, partner, low_edge, high_edge, partner_edge)
    gram, back_tiles = pl.pallas_call(
        cross_kernel,
        out_shape=(
            jax.ShapeDtypeStruct((2 * vecs, vecs), jnp.float32),
            jax.ShapeDtypeStruct((4 * rows // LANES, OCT, LANES), jnp.float32),
        ),
        in_specs=[vmem()] * 3,
        out_specs=(vmem(),) * 2,
        compiler_params=params(8),
        cost_estimate=cost(1),
        name="cross",
    )(back.reshape(4 * harm_size, LANES), cols, gram)
    total = spread_sum(gram.reshape(4, LANES), PLANE)
    image = pl.pallas_call(
        image_kernel,
        out_shape=block,
        in_specs=[vmem()] * 3,
        out_specs=vmem(),
        compiler_params=params(8),
        cost_estimate=cost(20),
        name="image",
    )(inv, adj, back_tiles)
    total = spread_sum(total, ("z",))
    return (image, total.reshape(2, vecs, vecs))


def solution(mesh):
    shape = (4, 16, 4, 2)
    mesh = jax.sharding.Mesh(mesh.devices.reshape(shape), ("y", "z", "x", "core"))
    in_specs = (P(HARM, None, GRP), P(GRP), P(GRP), P(GRP), P(), P(None, GRP, None))
    out_specs = (P(HARM, None, GRP), P())
    return jax.shard_map(local, mesh=mesh, in_specs=in_specs, out_specs=out_specs, check_vma=False)
```

time: 438 us -> 107 us (0.24)
  waiting for transfers between devices: 131 us -> 24.8 us
  other arithmetic: 105 us -> 0.15 us
  blocking collectives: 109 us -> 16.4 us
  local copies, waits for them, and re-layouts: 38.3 us -> 5.11 us
  starting transfers between devices: 12.5 us -> 41.3 us
  matrix products: 25.3 us -> 0 us
  Pallas kernels: 0 us -> 17 us
  between operations: 14.9 us -> 1.46 us
    psum x1 -> x0, blocking collectives: 109 us -> none  [local(): first, second = lax.psum((first, second), ('harm', 'grp'))]
    all_gather x1 -> x0, waiting for transfers between devices: 103 us -> none  [local(): lax.all_gather(rows, 'harm', axis=0, tiled=True)]
    scatter-add x1 -> x0, other arithmetic: 97.1 us -> none  [local(): image = adjusted.at[:, :, attach].add(back)]
    ppermute x3 -> x4, waiting for transfers between devices: 27.6 us -> 0.01 us  [the longest x1 0.01 us: local(): lax.ppermute(vectors[:, :, -1:], GRP, [(i, i + 1) for i in range(ends)])]
    dot_general x4 -> x0, matrix products: 25.3 us -> none  [the longest x1 17.9 us: local(): jnp.einsum('bk,kvr->bvr', basis, lax.all_gather(rows, 'harm', axis=0, til...]
    all_to_all x0 -> x3, waiting for transfers between devices: none -> 24.8 us  [the longest x1 8.8 us: local(): recv = lax.all_to_all(packed.reshape(harm_size, 4, LANES), HARM, 0, 0)]
    all_to_all x0 -> x3, starting transfers between devices: none -> 24.8 us  [the longest x1 15.8 us: local(): recv = lax.all_to_all(packed.reshape(harm_size, 4, LANES), HARM, 0, 0)]
    unnamed x12 -> x16, local copies, waits for them, and re-layouts: 21.1 us -> 2.85 us
  transfers between devices with their start and end apart: 4 -> 7, of which waited for: 2 -> 3; matrix products, arithmetic and copies ran while one was open for 3% -> 1% of each run, Pallas kernels for 0% -> 15%
where the time goes in v2:
time: 107 us; the launch traced here: 106 us
  starting transfers between devices  41.3 us (39%)
  waiting for transfers between devices  24.8 us (23%)
  Pallas kernels  17 us (16%)
  blocking collectives  16.4 us (15%)
  local copies, waits for them, and re-layouts  5.11 us (5%)
  between operations  1.46 us (1%)
    all_to_all x1, blocking collectives, spread_sum(): lax.all_to_all(jnp.broadcast_to(part[None], (count,) + part.shape), axes,...  16.4 us
    all_to_all x1, starting transfers between devices, local(): recv = lax.all_to_all(packed.reshape(harm_size, 4, LANES), HARM, 0, 0)  15.8 us
    all_to_all x1, waiting for transfers between devices, local(): recv = lax.all_to_all(packed.reshape(harm_size, 4, LANES), HARM, 0, 0)  8.8 us
    all_to_all x1, waiting for transfers between devices, local(): back = lax.all_to_all(back.reshape(harm_size, 4, LANES), HARM, 0, 0)  8.4 us
    all_to_all x1, waiting for transfers between devices, spread_sum(): lax.all_to_all(jnp.broadcast_to(part[None], (count,) + part.shape), axes,...  7.58 us
    ppermute x1, starting transfers between devices, local(): partner = lax.ppermute(vectors, HARM, to_partner)  5.65 us
    all_to_all x1, starting transfers between devices, local(): back = lax.all_to_all(back.reshape(harm_size, 4, LANES), HARM, 0, 0)  5.43 us
    pallas_call x1, Pallas kernels, local(): pl.pallas_call(adjust_kernel, out_shape=(block, jax.ShapeDtypeStruct((2 *...  5.41 us
  transfers between devices with their start and end apart: 7, of which 3 were waited for; matrix products, arithmetic and copies ran while one was open for 1% of the time, Pallas kernels for 15%

profile of v2, /device:TPU:1, one launch (start us, length us, event | category | flops | bytes accessed | tf_op | source)
XLA Modules:
  0.0 106.2 jit_solution(17058263462401657200)
XLA Ops:
  0.6 0.0 copy-start.4
  0.6 5.7 %collective-permute-start = (f32[2,16,8192]{2,1,0:T(8,128)}, f32[2,16,8192]{2,1,0:T(8,128)S(1)}, u32[]{:S(2)}, u32[]{:S(2)}) collective-permute-start(f32[2,16,8192]{2,1,0:T(8,128)} %v_ref.3), channel_id=1, source_target_pairs={{0,256},{8,264},{16,272},{24,280},{32,288},{40,296},{48,304},{56,3... | collective-permute-start | bytes 3145736 | tf_op jit(solution)/shard_map/ppermute | solution.py:298
  6.3 0.8 fusion
  7.1 3.9 %collective-permute-start.1 = (f32[2,16,1]{2,1,0:T(8,128)S(1)}, f32[2,16,1]{2,1,0:T(8,128)S(1)}, u32[]{:S(2)}, u32[]{:S(2)}) collective-permute-start(f32[2,16,1]{2,1,0:T(8,128)S(1)} %get-tuple-element.17), channel_id=1, source_target_pairs={{0,1},{1,2},{2,3},{3,4},{4,5},{5,6},{6,7},{8,9},{9,10},{10,11},{11... | collective-permute-start | bytes 392 | tf_op jit(solution)/shard_map/ppermute | solution.py:300
  11.1 2.4 %collective-permute-start.2 = (f32[2,16,1]{2,1,0:T(8,128)S(1)}, f32[2,16,1]{2,1,0:T(8,128)S(1)}, u32[]{:S(2)}, u32[]{:S(2)}) collective-permute-start(f32[2,16,1]{2,1,0:T(8,128)S(1)} %get-tuple-element.16), channel_id=1, source_target_pairs={{1,0},{2,1},{3,2},{4,3},{5,4},{6,5},{7,6},{9,8},{10,9},{11,10},{12... | collective-permute-start | bytes 392 | tf_op jit(solution)/shard_map/ppermute | solution.py:301
  13.5 0.0 copy-done.4
  13.5 0.0 copy-start
  13.5 1.2 %copy-done = f32[2,16,8192]{2,1,0:T(8,128)S(1)} copy-done((f32[2,16,8192]{2,1,0:T(8,128)S(1)}, f32[2,16,8192]{2,1,0:T(8,128)}, u32[]{:S(2)}) %copy-start) | copy-done | bytes 1048600
  14.7 4.5 %gather.1 = f32[256,128]{1,0:T(8,128)} custom-call(s32[1024]{0:T(1024)S(1)} %copy-done.4, f32[2,16,8192]{2,1,0:T(8,128)S(1)} %copy-done), custom_call_target="tpu_custom_call" | custom-call | flops 5000000000 | tf_op jit(solution)/shard_map/gather/pallas_call | solution.py:304
  19.2 15.8 %all-to-all-start = ((f32[64,4,128]{2,1,0:T(4,128)}), f32[64,4,128]{2,1,0:T(4,128)S(1)}, u32[]{:S(2)}, u32[]{:S(2)}) async-start(f32[64,4,128]{2,1,0:T(4,128)} %bitcast.3), calls=%async_computation | async-start | bytes 262144 | tf_op jit(solution)/shard_map/all_to_all | solution.py:314
  35.7 0.0 collective-permute-done.1.low_ref
  35.7 0.0 collective-permute-done.2.high_ref
  35.8 0.1 pad_maximum_fusion
  35.8 4.5 %collective-permute-start.3 = (f32[2,16,2]{2,1,0:T(8,128)S(1)}, f32[2,16,2]{2,1,0:T(8,128)S(1)}, u32[]{:S(2)}, u32[]{:S(2)}) collective-permute-start(f32[2,16,2]{2,1,0:T(8,128)S(1)} %pad_maximum_fusion), channel_id=1, source_target_pairs={{0,256},{8,264},{16,272},{24,280},{32,288},{40,296},{48,304},{56,3... | collective-permute-start | bytes 776 | tf_op jit(solution)/shard_map/ppermute | solution.py:302
  40.4 0.0 collective-permute-done.partner_ref.p_ref
  40.4 0.0 copy-start.5
  40.4 0.6 copy-done.5
  41.0 0.0 copy-start.2
  41.0 0.4 tables.1
  41.5 8.8 %all-to-all-done = f32[64,4,128]{2,1,0:T(4,128)S(1)} async-done(((f32[64,4,128]{2,1,0:T(4,128)}), f32[64,4,128]{2,1,0:T(4,128)S(1)}, u32[]{:S(2)}, u32[]{:S(2)}) %all-to-all-start) | async-done | bytes 131104 | tf_op jit(solution)/shard_map/all_to_all | solution.py:314
  50.3 0.0 copy-done.2
  50.3 0.0 copy-start.1
  50.3 1.8 %blades.1 = f32[256,128]{1,0:T(8,128)} custom-call(s32[1]{0:T(128)S(6)} %copy.15.live_ref, f32[256,128]{1,0:T(8,128)S(1)} %bitcast.8, f32[1024,128]{1,0:T(8,128)S(1)} %bitcast.10, f32[128,128]{1,0:T(8,128)S(1)} %get-tuple-element.11.basis_ref), custom_call_target="tpu_custom_call" | custom-call | flops 4000000000 | tf_op jit(solution)/shard_map/blades/pallas_call | solution.py:328
  52.1 0.0 copy-start.3
  52.1 5.4 %all-to-all-start.1 = ((f32[64,4,128]{2,1,0:T(4,128)}), f32[64,4,128]{2,1,0:T(4,128)S(1)}, u32[]{:S(2)}, u32[]{:S(2)}) async-start(f32[64,4,128]{2,1,0:T(4,128)} %bitcast.6), calls=%async_computation.1 | async-start | bytes 262144 | tf_op jit(solution)/shard_map/all_to_all | solution.py:337
  57.5 0.0 collective-permute-done.3.p_edge_ref
  57.5 0.0 copy-done.1
  57.6 0.0 copy-done.3
  57.6 5.4 %adjust.1 = (f32[2,16,8192]{2,1,0:T(8,128)S(1)}, f32[32,16]{1,0:T(8,128)S(1)}, f32[64,1024]{1,0:T(8,128)S(1)}) custom-call(s32[64]{0:T(128)S(1)} %copy-done.5, s32[1024]{0:T(1024)S(1)} %copy-done.4, f32[64,128]{1,0:T(8,128)S(1)} %bitcast.11, f32[2,16,8192]{2,1,0:T(8,128)S(1)} %copy-done.1, f32[2,16,8192]{2,1,0:T(8,128)S(1)} %collective-permute-done.partner_ref.p_ref, ...), custom_call_target="tpu_custom_call" | custom-call | flops 40000000000 | tf_op jit(solution)/shard_map/adjust/pallas_call | solution.py:339
  63.0 0.0 copy-start.6
  63.0 1.0 copy-done.6
  64.0 8.4 %all-to-all-done.1 = f32[64,4,128]{2,1,0:T(4,128)S(1)} async-done(((f32[64,4,128]{2,1,0:T(4,128)}), f32[64,4,128]{2,1,0:T(4,128)S(1)}, u32[]{:S(2)}, u32[]{:S(2)}) %all-to-all-start.1) | async-done | bytes 131104 | tf_op jit(solution)/shard_map/all_to_all | solution.py:337
  72.4 0.0 copy-start.7
  72.4 1.0 cross.1
  73.3 0.1 broadcast_in_dim.6
  73.5 16.4 %all_to_all.20 = f32[32,4,128]{2,1,0:T(4,128)S(1)} all-to-all(f32[32,4,128]{2,1,0:T(4,128)S(1)} %broadcast_in_dim.14), channel_id=1, replica_groups=mesh['y'=4,'z'=16,'x'=4,'core'=2] {'y','x','core'}, dimensions={0} | all-to-all | bytes 131072 | tf_op jit(solution)/shard_map/all_to_all | solution.py:285
  89.9 0.6 broadcast_in_dim.15
  90.5 3.5 %all-to-all-start.3 = ((f32[16,4,128]{2,1,0:T(4,128)}), f32[16,4,128]{2,1,0:T(4,128)S(1)}, u32[]{:S(2)}, u32[]{:S(2)}) async-start(f32[16,4,128]{2,1,0:T(4,128)} %broadcast_in_dim.15), calls=%async_computation.3 | async-start | bytes 65536 | tf_op jit(solution)/shard_map/all_to_all | solution.py:285
  94.0 0.0 copy-done.7
  94.0 3.9 %image.1 = f32[2,16,8192]{2,1,0:T(8,128)} custom-call(s32[2,64,128]{2,1,0:T(8,128)S(1)} %get-tuple-element.9.inv_ref, f32[2,16,8192]{2,1,0:T(8,128)S(1)} %copy-done.7, f32[32,8,128]{2,1,0:T(8,128)S(1)} %get-tuple-element.14.back_ref), custom_call_target="tpu_custom_call" | custom-call | flops 20000000000 | tf_op jit(solution)/shard_map/image/pallas_call | solution.py:366
  97.9 7.6 %all-to-all-done.3 = f32[16,4,128]{2,1,0:T(4,128)S(1)} async-done(((f32[16,4,128]{2,1,0:T(4,128)}), f32[16,4,128]{2,1,0:T(4,128)S(1)}, u32[]{:S(2)}, u32[]{:S(2)}) %all-to-all-start.3) | async-done | bytes 32800 | tf_op jit(solution)/shard_map/all_to_all | solution.py:285
  105.5 0.7 reshape.41
  (3 shorter events, 0.1 us)
Async XLA Ops:
  0.6 12.9 %copy-start.4 = (s32[1024]{0:T(1024)S(1)}, s32[1024]{0:T(1024)}, u32[]{:S(2)}) copy-start(s32[1024]{0:T(1024)} %attach_ref.3) | copy-start | bytes 12292
  0.6 39.7 %collective-permute-start = (f32[2,16,8192]{2,1,0:T(8,128)}, f32[2,16,8192]{2,1,0:T(8,128)S(1)}, u32[]{:S(2)}, u32[]{:S(2)}) collective-permute-start(f32[2,16,8192]{2,1,0:T(8,128)} %v_ref.3), channel_id=1, source_target_pairs={{0,256},{8,264},{16,272},{24,280},{32,288},{40,296},{48,304},{56,3... | collective-permute-start | bytes 3145736 | tf_op jit(solution)/shard_map/ppermute | solution.py:298
  7.1 28.6 %collective-permute-start.1 = (f32[2,16,1]{2,1,0:T(8,128)S(1)}, f32[2,16,1]{2,1,0:T(8,128)S(1)}, u32[]{:S(2)}, u32[]{:S(2)}) collective-permute-start(f32[2,16,1]{2,1,0:T(8,128)S(1)} %get-tuple-element.17), channel_id=1, source_target_pairs={{0,1},{1,2},{2,3},{3,4},{4,5},{5,6},{6,7},{8,9},{9,10},{10,11},{11... | collective-permute-start | bytes 392 | tf_op jit(solution)/shard_map/ppermute | solution.py:300
  11.1 24.6 %collective-permute-start.2 = (f32[2,16,1]{2,1,0:T(8,128)S(1)}, f32[2,16,1]{2,1,0:T(8,128)S(1)}, u32[]{:S(2)}, u32[]{:S(2)}) collective-permute-start(f32[2,16,1]{2,1,0:T(8,128)S(1)} %get-tuple-element.16), channel_id=1, source_target_pairs={{1,0},{2,1},{3,2},{4,3},{5,4},{6,5},{7,6},{9,8},{10,9},{11,10},{12... | collective-permute-start | bytes 392 | tf_op jit(solution)/shard_map/ppermute | solution.py:301
  13.5 1.2 %copy-start = (f32[2,16,8192]{2,1,0:T(8,128)S(1)}, f32[2,16,8192]{2,1,0:T(8,128)}, u32[]{:S(2)}) copy-start(f32[2,16,8192]{2,1,0:T(8,128)} %v_ref.3) | copy-start | bytes 3145732
  19.2 31.0 %all-to-all-start = ((f32[64,4,128]{2,1,0:T(4,128)}), f32[64,4,128]{2,1,0:T(4,128)S(1)}, u32[]{:S(2)}, u32[]{:S(2)}) async-start(f32[64,4,128]{2,1,0:T(4,128)} %bitcast.3), calls=%async_computation | async-start | bytes 262144 | tf_op jit(solution)/shard_map/all_to_all | solution.py:314
  35.8 21.7 %collective-permute-start.3 = (f32[2,16,2]{2,1,0:T(8,128)S(1)}, f32[2,16,2]{2,1,0:T(8,128)S(1)}, u32[]{:S(2)}, u32[]{:S(2)}) collective-permute-start(f32[2,16,2]{2,1,0:T(8,128)S(1)} %pad_maximum_fusion), channel_id=1, source_target_pairs={{0,256},{8,264},{16,272},{24,280},{32,288},{40,296},{48,304},{56,3... | collective-permute-start | bytes 776 | tf_op jit(solution)/shard_map/ppermute | solution.py:302
  40.4 0.7 copy-start.5
  41.0 9.3 %copy-start.2 = (f32[128,1,1024]{2,1,0:T(1,128)S(1)}, f32[128,1,1024]{2,1,0:T(1,128)}, u32[]{:S(2)}) copy-start(f32[128,1,1024]{2,1,0:T(1,128)} %param.11) | copy-start | bytes 1572868
  50.3 7.3 %copy-start.1 = (f32[2,16,8192]{2,1,0:T(8,128)S(1)}, f32[2,16,8192]{2,1,0:T(8,128)}, u32[]{:S(2)}) copy-start(f32[2,16,8192]{2,1,0:T(8,128)} %v_ref.3) | copy-start | bytes 3145732
  52.1 5.5 %copy-start.3 = (f32[8192]{0:T(1024)S(1)}, f32[8192]{0:T(1024)}, u32[]{:S(2)}) copy-start(f32[8192]{0:T(1024)} %param.7) | copy-start | bytes 98308
  52.1 20.3 %all-to-all-start.1 = ((f32[64,4,128]{2,1,0:T(4,128)}), f32[64,4,128]{2,1,0:T(4,128)S(1)}, u32[]{:S(2)}, u32[]{:S(2)}) async-start(f32[64,4,128]{2,1,0:T(4,128)} %bitcast.6), calls=%async_computation.1 | async-start | bytes 262144 | tf_op jit(solution)/shard_map/all_to_all | solution.py:337
  63.0 1.0 copy-start.6
  72.4 21.6 %copy-start.7 = (f32[2,16,8192]{2,1,0:T(8,128)S(1)}, f32[2,16,8192]{2,1,0:T(8,128)}, u32[]{:S(2)}) copy-start(f32[2,16,8192]{2,1,0:T(8,128)} %copy-done.6) | copy-start | bytes 3145732
  90.5 15.0 %all-to-all-start.3 = ((f32[16,4,128]{2,1,0:T(4,128)}), f32[16,4,128]{2,1,0:T(4,128)S(1)}, u32[]{:S(2)}, u32[]{:S(2)}) async-start(f32[16,4,128]{2,1,0:T(4,128)} %broadcast_in_dim.15), calls=%async_computation.3 | async-start | bytes 65536 | tf_op jit(solution)/shard_map/all_to_all | solution.py:285

commit v3 on v2

--- a/solution.py
+++ b/solution.py
@@ -1,3 +1,4 @@
+import functools
 import math
 
 import jax
@@ -70,7 +71,7 @@
 
 
 def fetch(attach_ref, t_ref, g_ref):
-    group = 16
+    group = 64
 
     def step(n, carry):
         for u in range(group):
@@ -81,13 +82,16 @@
     lax.fori_loop(0, attach_ref.shape[0] // group, step, 0)
 
 
-def gather_kernel(attach_ref, v_ref, out_ref, t_ref, g_ref):
+def gather_kernel(attach_ref, v_ref, out_ref, head_ref, tail_ref, t_ref, g_ref):
+    head_ref[...] = v_ref[:, :, :1]
+    tail_ref[...] = v_ref[:, :, v_ref.shape[2] - 1 :]
+
     def step(i, carry):
         here = pl.ds(pl.multiple_of(i * LANES, LANES), LANES)
         t_ref[here, :] = jnp.concatenate([v_ref[k2, o, here] for k2, o in OCTETS], axis=0).T
         return carry
 
-    lax.fori_loop(0, v_ref.shape[2] // LANES, step, 0, unroll=8)
+    lax.fori_loop(0, v_ref.shape[2] // LANES, step, 0, unroll=32)
     fetch(attach_ref, t_ref, g_ref)
     owners = out_ref.shape[0] // 4
     part = iota((owners, LANES), 1) // 32
@@ -137,32 +141,38 @@
     return v, lo, hi
 
 
-def adjust_kernel(pair_ref, attach_ref, stiff_ref, v_ref, p_ref, low_ref, high_ref, p_edge_ref, adj_ref, gram_ref, cols_ref, t_ref, g_ref):
-    tiles, vecs, per = stiff_ref.shape[0], v_ref.shape[1], 4
+def adjusted(pair_ref, stiff_ref, v_ref, p_ref, edge_refs):
+    tiles = stiff_ref.shape[0]
     terms = [own_terms(pair_ref, k2) for k2 in range(2)]
-
-    def edge(ref, k2, o, n):
-        return jnp.broadcast_to(ref[k2, o, n : n + 1], (OCT, LANES))
-
-    low = [edge(low_ref, k2, o, 0) for k2, o in OCTETS]
-    high = [edge(high_ref, k2, o, 0) for k2, o in OCTETS]
-    p_low = [edge(p_edge_ref, k2, o, 0) for k2, o in OCTETS]
-    p_high = [edge(p_edge_ref, k2, o, 1) for k2, o in OCTETS]
+    if edge_refs is None:
+        low = high = p_low = p_high = [jnp.zeros((OCT, LANES), jnp.float32)] * 4
+    else:
+        low, high = [[jnp.broadcast_to(ref[k2, o, :], (OCT, LANES)) for k2, o in OCTETS] for ref in edge_refs[:2]]
+        p_low, p_high = [[jnp.broadcast_to(edge_refs[2][k2, o, n : n + 1], (OCT, LANES)) for k2, o in OCTETS] for n in range(2)]
+
+    def at(i):
+        stiff = jnp.broadcast_to(stiff_ref[pl.ds(i, 1), :], (OCT, LANES))
+        v_tile, w_tile = [], []
+        for j, (k2, o) in enumerate(OCTETS):
+            v, lo, hi = shifted(v_ref, k2, o, i, tiles, low[j], high[j])
+            _, p_lo, p_hi = shifted(p_ref, k2, o, i, tiles, p_low[j], p_high[j])
+            v_tile.append(v)
+            w_tile.append((terms[k2][0] + stiff) * v - lo - hi + terms[k2][1] * (p_hi - p_lo))
+        return v_tile, w_tile
+
+    return at
+
+
+def adjust_kernel(pair_ref, attach_ref, stiff_ref, v_ref, p_ref, gram_ref, cols_ref, t_ref, g_ref):
+    tiles, vecs, per = stiff_ref.shape[0], v_ref.shape[1], 8
+    at = adjusted(pair_ref, stiff_ref, v_ref, p_ref, None)
 
     def step(g, gram):
         vs, ws = [], []
         for t in range(per):
             i = g * per + t
+            v_tile, w_tile = at(i)
             here = pl.ds(pl.multiple_of(i * LANES, LANES), LANES)
-            stiff = jnp.broadcast_to(stiff_ref[pl.ds(i, 1), :], (OCT, LANES))
-            v_tile, w_tile = [], []
-            for j, (k2, o) in enumerate(OCTETS):
-                v, lo, hi = shifted(v_ref, k2, o, i, tiles, low[j], high[j])
-                _, p_lo, p_hi = shifted(p_ref, k2, o, i, tiles, p_low[j], p_high[j])
-                w = (terms[k2][0] + stiff) * v - lo - hi + terms[k2][1] * (p_hi - p_lo)
-                adj_ref[k2, o, here] = w
-                v_tile.append(v)
-                w_tile.append(w)
             t_ref[here, :] = jnp.concatenate(v_tile + w_tile, axis=0).T
             vs.append(jnp.concatenate(v_tile, axis=0))
             ws.append(jnp.concatenate(w_tile, axis=0))
@@ -174,7 +184,7 @@
             gram = gram + lax.dot_general(left, jnp.concatenate(w3, axis=0), NT, preferred_element_type=jnp.float32)
         return gram
 
-    total = lax.fori_loop(0, tiles // per, step, jnp.zeros((6 * vecs, 3 * vecs), jnp.float32), unroll=2)
+    total = lax.fori_loop(0, tiles // per, step, jnp.zeros((6 * vecs, 3 * vecs), jnp.float32))
     for n in range(2):
         gram = jnp.zeros((vecs, vecs), jnp.float32)
         for a in range(3):
@@ -183,12 +193,19 @@
                 gram = gram + total[at : at + vecs, b * vecs : (b + 1) * vecs]
         gram_ref[n * vecs : (n + 1) * vecs, :] = gram
     fetch(attach_ref, t_ref, g_ref)
-    for c in range(cols_ref.shape[1] // LANES):
+    rows, last = g_ref.shape[0], t_ref.shape[0] - 1
+    for c in range(rows // LANES):
         here = slice(LANES * c, LANES * (c + 1))
         cols_ref[:, here] = g_ref[here, :].T
-
-
-def blade_kernel(live_ref, recv_ref, mistune_ref, basis_ref, out_ref):
+    g_ref[:LANES, :] = jnp.zeros((LANES, g_ref.shape[1]), jnp.float32)
+    g_ref[0:1, :] = t_ref[0:1, :]
+    g_ref[1:2, :] = t_ref[last : last + 1, :]
+    cols_ref[:, rows:] = g_ref[:LANES, :].T
+
+
+def blade_kernel(live_ref, recv_ref, mistune_ref, basis_ref, low_ref, high_ref, out_ref, edge_ref):
+    edge_ref[:, :, 0:1] = low_ref[...]
+    edge_ref[:, :, 1:2] = high_ref[...]
     me, live = harm_index(), live_ref[0]
     owners = out_ref.shape[0] // 4
     blades = 2 * owners
@@ -224,38 +241,49 @@
         out_ref[pl.ds(j, owners, stride=4), :] = turned[owners * k2 : owners * (k2 + 1), LANES * vh : LANES * (vh + 1)]
 
 
-def cross_kernel(recv_ref, cols_ref, gram_ref, total_ref, back_ref):
-    vecs, chunks = gram_ref.shape[1], cols_ref.shape[1] // LANES
+def cross_kernel(width, pair_ref, attach_ref, recv_ref, cols_ref, gram_ref, low_ref, high_ref, p_edge_ref, total_ref, back_ref):
+    vecs, rows = gram_ref.shape[1], attach_ref.shape[1]
+    chunks = rows // LANES
     tiles = [[swap_blocks(recv_ref[pl.ds(4 * OCT * c + j, OCT, stride=4), :]) for c in range(chunks)] for j in range(4)]
     total = gram_ref[...]
+    attach = attach_ref[...]
+    at_first, at_last = attach == 0, attach == width - 1
+    lane = iota((vecs, LANES), 1)
     for k2 in range(2):
+        coup = own_terms(pair_ref, k2)[1][0:1, 0:1]
         both = []
         for j in (2 * k2, 2 * k2 + 1):
             for c in range(chunks):
                 back_ref[4 * c + j] = tiles[j][c]
             both.append(jnp.concatenate(tiles[j], axis=1))
         back = jnp.concatenate(both, axis=0)
-        left = jnp.concatenate(
-            [cols_ref[vecs * k2 : vecs * (k2 + 1), :], cols_ref[vecs * (k2 + 2) : vecs * (k2 + 3), :] + 0.5 * back], axis=0
-        )
-        term = dot_f32(left, back, NT)
-        twice = dot_f32(back, left[vecs:], NT)
+        first = -low_ref[k2] - coup * p_edge_ref[k2, :, 0:1]
+        last = -high_ref[k2] + coup * p_edge_ref[k2, :, 1:2]
+        outer = jnp.where(lane == 0, first, jnp.where(lane == 1, last, 0.0))
+        at_rows = jnp.where(at_first, first, jnp.where(at_last, last, 0.0))
+        more = jnp.concatenate([back, outer], axis=1)
+        adj = cols_ref[vecs * (k2 + 2) : vecs * (k2 + 3), :] + jnp.concatenate([at_rows, jnp.zeros_like(outer)], axis=1)
+        left = jnp.concatenate([cols_ref[vecs * k2 : vecs * (k2 + 1), :], adj + 0.5 * more], axis=0)
+        term = dot_f32(left, more, NT)
+        twice = dot_f32(more, left[vecs:], NT)
         total = total + term + jnp.concatenate([jnp.zeros_like(twice), twice], axis=0)
     total_ref[...] = total
 
 
-def image_kernel(inv_ref, adj_ref, back_ref, image_ref):
+def image_kernel(pair_ref, inv_ref, stiff_ref, v_ref, p_ref, low_ref, high_ref, p_edge_ref, back_ref, image_ref):
     tiles, chunks = inv_ref.shape[1], back_ref.shape[0] // 4
+    at = adjusted(pair_ref, stiff_ref, v_ref, p_ref, (low_ref, high_ref, p_edge_ref))
 
     def step(i, carry):
         here = pl.ds(pl.multiple_of(i * LANES, LANES), LANES)
         chunk = jnp.broadcast_to(inv_ref[0, pl.ds(i, 1), :], (OCT, LANES))
         index = jnp.broadcast_to(inv_ref[1, pl.ds(i, 1), :], (OCT, LANES))
+        _, w_tile = at(i)
         for j, (k2, o) in enumerate(OCTETS):
             back = jnp.zeros((OCT, LANES), jnp.float32)
             for c in range(chunks):
                 back = jnp.where(chunk == c + 1, pick(back_ref[4 * c + j], index), back)
-            image_ref[k2, o, here] = adj_ref[k2, o, here] + back
+            image_ref[k2, o, here] = w_tile[j] + back
         return carry
 
     lax.fori_loop(0, tiles, step, 0, unroll=8)
@@ -296,22 +324,21 @@
     half = harm_size // 2
     to_partner = [(i, i ^ half) for i in range(harm_size)]
     partner = lax.ppermute(vectors, HARM, to_partner)
-    ends = grp_size - 1
-    low_edge = lax.ppermute(vectors[:, :, -1:], GRP, [(i, i + 1) for i in range(ends)])
-    high_edge = lax.ppermute(vectors[:, :, :1], GRP, [(i + 1, i) for i in range(ends)])
-    partner_edge = lax.ppermute(jnp.concatenate([low_edge, high_edge], axis=2), HARM, to_partner)
-
-    packed = pl.pallas_call(
+    edge = jax.ShapeDtypeStruct((slot_count, vecs, 1), jnp.float32)
+    packed, head, tail = pl.pallas_call(
         gather_kernel,
-        out_shape=packed_rows,
+        out_shape=(packed_rows, edge, edge),
         in_specs=[smem(), vmem()],
-        out_specs=vmem(),
+        out_specs=(vmem(),) * 3,
         scratch_shapes=[pltpu.VMEM((width, 2 * vecs), jnp.float32), pltpu.VMEM((rows, 2 * vecs), jnp.float32)],
         compiler_params=params(16),
         cost_estimate=cost(5),
         name="gather",
     )(attach, vectors)
     recv = lax.all_to_all(packed.reshape(harm_size, 4, LANES), HARM, 0, 0)
+    ends = grp_size - 1
+    low_edge = lax.ppermute(tail, GRP, [(i, i + 1) for i in range(ends)])
+    high_edge = lax.ppermute(head, GRP, [(i + 1, i) for i in range(ends)])
 
     basis, inv = pl.pallas_call(
         table_kernel,
@@ -325,53 +352,54 @@
         cost_estimate=cost(60),
         name="tables",
     )(pair_harm.reshape(1, -1), attach.reshape(1, -1), partner)
-    back = pl.pallas_call(
+    back, own_edge = pl.pallas_call(
         blade_kernel,
-        out_shape=packed_rows,
-        in_specs=[smem()] + [vmem()] * 3,
-        out_specs=vmem(),
+        out_shape=(packed_rows, jax.ShapeDtypeStruct((slot_count, vecs, 2), jnp.float32)),
+        in_specs=[smem()] + [vmem()] * 5,
+        out_specs=(vmem(),) * 2,
         compiler_params=params(16),
         cost_estimate=cost(4),
         name="blades",
-    )(live, recv.reshape(4 * harm_size, LANES), mistune.reshape(-1, LANES), basis)
+    )(live, recv.reshape(4 * harm_size, LANES), mistune.reshape(-1, LANES), basis, low_edge, high_edge)
     back = lax.all_to_all(back.reshape(harm_size, 4, LANES), HARM, 0, 0)
-
-    adj, gram, cols = pl.pallas_call(
+    partner_edge = lax.ppermute(own_edge, HARM, to_partner)
+
+    stiff = stiffness.reshape(-1, LANES)
+    gram, cols = pl.pallas_call(
         adjust_kernel,
         out_shape=(
-            block,
             jax.ShapeDtypeStruct((2 * vecs, vecs), jnp.float32),
-            jax.ShapeDtypeStruct((4 * vecs, rows), jnp.float32),
+            jax.ShapeDtypeStruct((4 * vecs, rows + LANES), jnp.float32),
         ),
-        in_specs=[smem(), smem()] + [vmem()] * 6,
-        out_specs=(vmem(),) * 3,
+        in_specs=[smem(), smem()] + [vmem()] * 3,
+        out_specs=(vmem(),) * 2,
         scratch_shapes=[pltpu.VMEM((width, 4 * vecs), jnp.float32), pltpu.VMEM((rows, 4 * vecs), jnp.float32)],
         compiler_params=params(16),
         cost_estimate=cost(40),
         name="adjust",
-    )(pair_harm, attach, stiffness.reshape(-1, LANES), vectors, partner, low_edge, high_edge, partner_edge)
+    )(pair_harm, attach, stiff, vectors, partner)
     gram, back_tiles = pl.pallas_call(
-        cross_kernel,
+        functools.partial(cross_kernel, width),
         out_shape=(
             jax.ShapeDtypeStruct((2 * vecs, vecs), jnp.float32),
             jax.ShapeDtypeStruct((4 * rows // LANES, OCT, LANES), jnp.float32),
         ),
-        in_specs=[vmem()] * 3,
+        in_specs=[smem()] + [vmem()] * 7,
         out_specs=(vmem(),) * 2,
         compiler_params=params(8),
         cost_estimate=cost(1),
         name="cross",
-    )(back.reshape(4 * harm_size, LANES), cols, gram)
+    )(pair_harm, attach.reshape(1, -1), back.reshape(4 * harm_size, LANES), cols, gram, low_edge, high_edge, partner_edge)
     total = spread_sum(gram.reshape(4, LANES), PLANE)
     image = pl.pallas_call(
         image_kernel,
         out_shape=block,
-        in_specs=[vmem()] * 3,
+        in_specs=[smem()] + [vmem()] * 8,
         out_specs=vmem(),
         compiler_params=params(8),
         cost_estimate=cost(20),
         name="image",
-    )(inv, adj, back_tiles)
+    )(pair_harm, inv, stiff, vectors, partner, low_edge, high_edge, partner_edge, back_tiles)
     total = spread_sum(total, ("z",))
     return (image, total.reshape(2, vecs, vecs))
 

time: 107 us -> 104 us (0.972)
  waiting for transfers between devices: 24.8 us -> 17.6 us
  starting transfers between devices: 41.3 us -> 46.5 us
  Pallas kernels: 17 us -> 18.5 us
  blocking collectives: 16.4 us -> 14.9 us
  local copies, waits for them, and re-layouts: 5.11 us -> 3.97 us
    all_to_all x1, starting transfers between devices: 5.43 us -> 10.3 us  [local(): back = lax.all_to_all(back.reshape(harm_size, 4, LANES), HARM, 0, 0)]
    all_to_all x1, waiting for transfers between devices: 8.8 us -> 4.35 us  [local(): recv = lax.all_to_all(packed.reshape(harm_size, 4, LANES), HARM, 0, 0)]
    all_to_all x1, waiting for transfers between devices: 8.4 us -> 5.93 us  [local(): back = lax.all_to_all(back.reshape(harm_size, 4, LANES), HARM, 0, 0)]
    all_to_all x1, waiting for transfers between devices: 7.58 us -> 5.66 us  [spread_sum(): lax.all_to_all(jnp.broadcast_to(part[None], (count,) + part.shape), axes,...]
    ppermute x3, waiting for transfers between devices: 0.01 us -> 1.65 us  [the longest x1 1.65 us: local(): high_edge = lax.ppermute(head, GRP, [(i + 1, i) for i in range(ends)])]
    pallas_call x5, Pallas kernels: 16.6 us -> 18.1 us  [the longest x1 5.81 us: local(): pl.pallas_call(image_kernel, out_shape=block, in_specs=[smem()] + [vmem()...]
    all_to_all x1, blocking collectives: 16.4 us -> 14.9 us  [spread_sum(): lax.all_to_all(jnp.broadcast_to(part[None], (count,) + part.shape), axes,...]
    unnamed x16 -> x14, local copies, waits for them, and re-layouts: 2.85 us -> 2.57 us
  transfers between devices with their start and end apart: 7 -> 7, of which waited for: 3 -> 4; matrix products, arithmetic and copies ran while one was open for 1% -> 0% of each run, Pallas kernels for 15% -> 15%
where the time goes in v3:
time: 104 us; the launch traced here: 103 us
  starting transfers between devices  46.5 us (45%)
  Pallas kernels  18.5 us (18%)
  waiting for transfers between devices  17.6 us (17%)
  blocking collectives  14.9 us (14%)
  local copies, waits for them, and re-layouts  3.97 us (4%)
  between operations  1.43 us (1%)
    all_to_all x1, starting transfers between devices, local(): recv = lax.all_to_all(packed.reshape(harm_size, 4, LANES), HARM, 0, 0)  16.3 us
    all_to_all x1, blocking collectives, spread_sum(): lax.all_to_all(jnp.broadcast_to(part[None], (count,) + part.shape), axes,...  14.9 us
    all_to_all x1, starting transfers between devices, local(): back = lax.all_to_all(back.reshape(harm_size, 4, LANES), HARM, 0, 0)  10.3 us
    all_to_all x1, waiting for transfers between devices, local(): back = lax.all_to_all(back.reshape(harm_size, 4, LANES), HARM, 0, 0)  5.93 us
    pallas_call x1, Pallas kernels, local(): pl.pallas_call(image_kernel, out_shape=block, in_specs=[smem()] + [vmem()...  5.81 us
    all_to_all x1, waiting for transfers between devices, spread_sum(): lax.all_to_all(jnp.broadcast_to(part[None], (count,) + part.shape), axes,...  5.66 us
    ppermute x1, starting transfers between devices, local(): partner = lax.ppermute(vectors, HARM, to_partner)  5.65 us
    pallas_call x1, Pallas kernels, local(): pl.pallas_call(adjust_kernel, out_shape=(jax.ShapeDtypeStruct((2 * vecs,...  4.97 us
  transfers between devices with their start and end apart: 7, of which 4 were waited for; matrix products, arithmetic and copies ran while one was open for 0% of the time, Pallas kernels for 15%

profile of v3, /device:TPU:1, one launch (start us, length us, event | category | flops | bytes accessed | tf_op | source)
XLA Modules:
  0.0 103.0 jit_solution(1447548950047887291)
XLA Ops:
  0.6 5.7 %collective-permute-start = (f32[2,16,8192]{2,1,0:T(8,128)}, f32[2,16,8192]{2,1,0:T(8,128)S(1)}, u32[]{:S(2)}, u32[]{:S(2)}) collective-permute-start(f32[2,16,8192]{2,1,0:T(8,128)} %v_ref.5), channel_id=1, source_target_pairs={{0,256},{8,264},{16,272},{24,280},{32,288},{40,296},{48,304},{56,3... | collective-permute-start | bytes 3145736 | tf_op jit(solution)/shard_map/ppermute | solution.py:326
  6.3 0.0 copy-start
  6.3 1.2 %copy-done = f32[2,16,8192]{2,1,0:T(8,128)S(1)} copy-done((f32[2,16,8192]{2,1,0:T(8,128)S(1)}, f32[2,16,8192]{2,1,0:T(8,128)}, u32[]{:S(2)}) %copy-start) | copy-done | bytes 1048600
  7.5 0.0 copy-start.4
  7.5 0.7 copy-done.4
  8.2 3.9 %gather.1 = (f32[256,128]{1,0:T(8,128)}, f32[2,16,1]{2,1,0:T(8,128)S(1)}, f32[2,16,1]{2,1,0:T(8,128)S(1)}) custom-call(s32[1024]{0:T(1024)S(1)} %copy-done.4, f32[2,16,8192]{2,1,0:T(8,128)S(1)} %copy-done), custom_call_target="tpu_custom_call" | custom-call | flops 5000000000 | tf_op jit(solution)/shard_map/gather/pallas_call | solution.py:328
  12.1 16.3 %all-to-all-start = ((f32[64,4,128]{2,1,0:T(4,128)}), f32[64,4,128]{2,1,0:T(4,128)S(1)}, u32[]{:S(2)}, u32[]{:S(2)}) async-start(f32[64,4,128]{2,1,0:T(4,128)} %bitcast.3), calls=%async_computation | async-start | bytes 262144 | tf_op jit(solution)/shard_map/all_to_all | solution.py:338
  28.4 0.0 copy-start.5
  28.5 4.2 %collective-permute-start.1 = (f32[2,16,1]{2,1,0:T(8,128)S(1)}, f32[2,16,1]{2,1,0:T(8,128)S(1)}, u32[]{:S(2)}, u32[]{:S(2)}) collective-permute-start(f32[2,16,1]{2,1,0:T(8,128)S(1)} %get-tuple-element.14), channel_id=1, source_target_pairs={{0,1},{1,2},{2,3},{3,4},{4,5},{5,6},{6,7},{8,9},{9,10},{10,11},{11... | collective-permute-start | bytes 392 | tf_op jit(solution)/shard_map/ppermute | solution.py:340
  32.7 1.9 %collective-permute-start.2 = (f32[2,16,1]{2,1,0:T(8,128)S(1)}, f32[2,16,1]{2,1,0:T(8,128)S(1)}, u32[]{:S(2)}, u32[]{:S(2)}) collective-permute-start(f32[2,16,1]{2,1,0:T(8,128)S(1)} %get-tuple-element.15), channel_id=1, source_target_pairs={{1,0},{2,1},{3,2},{4,3},{5,4},{6,5},{7,6},{9,8},{10,9},{11,10},{12... | collective-permute-start | bytes 392 | tf_op jit(solution)/shard_map/ppermute | solution.py:341
  35.3 0.0 collective-permute-done.partner_ref.p_ref
  35.3 0.0 copy-start.6
  35.3 0.0 copy-done.5
  35.3 0.6 copy-done.6
  36.0 0.0 copy-start.2
  36.0 0.4 tables.1
  36.4 0.0 collective-permute-done.1.low_ref
  36.4 1.6 %collective-permute-done.2.high_ref = f32[2,16,1]{2,1,0:T(8,128)S(1)} collective-permute-done((f32[2,16,1]{2,1,0:T(8,128)S(1)}, f32[2,16,1]{2,1,0:T(8,128)S(1)}, u32[]{:S(2)}, u32[]{:S(2)}) %collective-permute-start.2) | collective-permute-done | bytes 160 | tf_op jit(solution)/shard_map/ppermute | solution.py:341
  38.1 4.3 %all-to-all-done = f32[64,4,128]{2,1,0:T(4,128)S(1)} async-done(((f32[64,4,128]{2,1,0:T(4,128)}), f32[64,4,128]{2,1,0:T(4,128)S(1)}, u32[]{:S(2)}, u32[]{:S(2)}) %all-to-all-start) | async-done | bytes 131104 | tf_op jit(solution)/shard_map/all_to_all | solution.py:338
  42.4 0.0 copy-done.2
  42.4 0.0 copy-start.1
  42.4 1.8 %blades.1 = (f32[256,128]{1,0:T(8,128)}, f32[2,16,2]{2,1,0:T(8,128)S(1)}) custom-call(s32[1]{0:T(128)S(6)} %copy.12.live_ref, f32[256,128]{1,0:T(8,128)S(1)} %bitcast.8, f32[1024,128]{1,0:T(8,128)S(1)} %bitcast.10, f32[128,128]{1,0:T(8,128)S(1)} %get-tuple-element.17.basis_ref, f32[2,16,1]{2,1,0:T(8,128)S(1)} %collective-permute-done.1.low_ref, ...), custom_call_target="tpu_custom_call" | custom-call | flops 4000000000 | tf_op jit(solution)/shard_map/blades/pallas_call | solution.py:355
  44.2 0.0 copy-start.3
  44.2 10.3 %all-to-all-start.1 = ((f32[64,4,128]{2,1,0:T(4,128)}), f32[64,4,128]{2,1,0:T(4,128)S(1)}, u32[]{:S(2)}, u32[]{:S(2)}) async-start(f32[64,4,128]{2,1,0:T(4,128)} %bitcast.6), calls=%async_computation.1 | async-start | bytes 262144 | tf_op jit(solution)/shard_map/all_to_all | solution.py:364
  54.6 4.5 %collective-permute-start.3 = (f32[2,16,2]{2,1,0:T(8,128)S(1)}, f32[2,16,2]{2,1,0:T(8,128)S(1)}, u32[]{:S(2)}, u32[]{:S(2)}) collective-permute-start(f32[2,16,2]{2,1,0:T(8,128)S(1)} %get-tuple-element.18), channel_id=1, source_target_pairs={{0,256},{8,264},{16,272},{24,280},{32,288},{40,296},{48,304},{56,3... | collective-permute-start | bytes 776 | tf_op jit(solution)/shard_map/ppermute | solution.py:365
  59.1 0.0 copy-done.1
  59.1 0.0 copy-done.3
  59.1 5.0 %adjust.1 = (f32[32,16]{1,0:T(8,128)S(1)}, f32[64,1152]{1,0:T(8,128)S(1)}) custom-call(s32[64]{0:T(128)S(1)} %copy-done.6, s32[1024]{0:T(1024)S(1)} %copy-done.5, f32[64,128]{1,0:T(8,128)S(1)} %bitcast.11, f32[2,16,8192]{2,1,0:T(8,128)S(1)} %copy-done.1, f32[2,16,8192]{2,1,0:T(8,128)S(1)} %collective-permute-done.partner_ref.p_ref), custom_call_target="tpu_custom_call" | custom-call | flops 40000000000 | tf_op jit(solution)/shard_map/adjust/pallas_call | solution.py:368
  64.1 0.0 collective-permute-done.3.p_edge_ref
  64.1 5.9 %all-to-all-done.1 = f32[64,4,128]{2,1,0:T(4,128)S(1)} async-done(((f32[64,4,128]{2,1,0:T(4,128)}), f32[64,4,128]{2,1,0:T(4,128)S(1)}, u32[]{:S(2)}, u32[]{:S(2)}) %all-to-all-start.1) | async-done | bytes 131104 | tf_op jit(solution)/shard_map/all_to_all | solution.py:364
  70.0 1.6 %cross.1 = (f32[32,16]{1,0:T(8,128)S(1)}, f32[32,8,128]{2,1,0:T(8,128)S(1)}) custom-call(s32[64]{0:T(128)S(1)} %copy-done.6, s32[1,1024]{1,0:T(1,128)S(1)} %bitcast.14, f32[256,128]{1,0:T(8,128)S(1)} %bitcast.9, f32[64,1152]{1,0:T(8,128)S(1)} %get-tuple-element.20.cols_ref, f32[32,16]{1,0:T(8,128)S(1)} %get-tuple-element.21.gram_ref, ...), custom_call_target="tpu_custom_call" | custom-call | flops 1000000000 | tf_op jit(solution)/shard_map/cross/pallas_call | solution.py:381
  71.6 0.1 broadcast_in_dim.6
  71.7 14.9 %all_to_all.20 = f32[32,4,128]{2,1,0:T(4,128)S(1)} all-to-all(f32[32,4,128]{2,1,0:T(4,128)S(1)} %broadcast_in_dim.14), channel_id=1, replica_groups=mesh['y'=4,'z'=16,'x'=4,'core'=2] {'y','x','core'}, dimensions={0} | all-to-all | bytes 131072 | tf_op jit(solution)/shard_map/all_to_all | solution.py:313
  86.7 0.6 broadcast_in_dim.15
  87.3 3.5 %all-to-all-start.3 = ((f32[16,4,128]{2,1,0:T(4,128)}), f32[16,4,128]{2,1,0:T(4,128)S(1)}, u32[]{:S(2)}, u32[]{:S(2)}) async-start(f32[16,4,128]{2,1,0:T(4,128)} %broadcast_in_dim.15), calls=%async_computation.3 | async-start | bytes 65536 | tf_op jit(solution)/shard_map/all_to_all | solution.py:313
  90.8 5.8 %image.1 = f32[2,16,8192]{2,1,0:T(8,128)} custom-call(s32[64]{0:T(128)S(1)} %copy-done.6, s32[2,64,128]{2,1,0:T(8,128)S(1)} %get-tuple-element.13.inv_ref, f32[64,128]{1,0:T(8,128)S(1)} %bitcast.12, f32[2,16,8192]{2,1,0:T(8,128)S(1)} %copy-done.1, f32[2,16,8192]{2,1,0:T(8,128)S(1)} %collective-permute-done.partner_ref.p_ref, ...), custom_call_target="tpu_custom_call" | custom-call | flops 20000000000 | tf_op jit(solution)/shard_map/image/pallas_call | solution.py:394
  96.6 5.7 %all-to-all-done.3 = f32[16,4,128]{2,1,0:T(4,128)S(1)} async-done(((f32[16,4,128]{2,1,0:T(4,128)}), f32[16,4,128]{2,1,0:T(4,128)S(1)}, u32[]{:S(2)}, u32[]{:S(2)}) %all-to-all-start.3) | async-done | bytes 32800 | tf_op jit(solution)/shard_map/all_to_all | solution.py:313
  102.3 0.7 reshape.42
  (3 shorter events, 0.1 us)
Async XLA Ops:
  0.6 34.7 %collective-permute-start = (f32[2,16,8192]{2,1,0:T(8,128)}, f32[2,16,8192]{2,1,0:T(8,128)S(1)}, u32[]{:S(2)}, u32[]{:S(2)}) collective-permute-start(f32[2,16,8192]{2,1,0:T(8,128)} %v_ref.5), channel_id=1, source_target_pairs={{0,256},{8,264},{16,272},{24,280},{32,288},{40,296},{48,304},{56,3... | collective-permute-start | bytes 3145736 | tf_op jit(solution)/shard_map/ppermute | solution.py:326
  6.3 1.2 %copy-start = (f32[2,16,8192]{2,1,0:T(8,128)S(1)}, f32[2,16,8192]{2,1,0:T(8,128)}, u32[]{:S(2)}) copy-start(f32[2,16,8192]{2,1,0:T(8,128)} %v_ref.5) | copy-start | bytes 3145732
  7.5 0.7 copy-start.4
  12.1 30.3 %all-to-all-start = ((f32[64,4,128]{2,1,0:T(4,128)}), f32[64,4,128]{2,1,0:T(4,128)S(1)}, u32[]{:S(2)}, u32[]{:S(2)}) async-start(f32[64,4,128]{2,1,0:T(4,128)} %bitcast.3), calls=%async_computation | async-start | bytes 262144 | tf_op jit(solution)/shard_map/all_to_all | solution.py:338
  28.4 6.9 %copy-start.5 = (s32[1024]{0:T(1024)S(1)}, s32[1024]{0:T(1024)}, u32[]{:S(2)}) copy-start(s32[1024]{0:T(1024)} %attach_ref.3) | copy-start | bytes 12292
  28.5 7.9 %collective-permute-start.1 = (f32[2,16,1]{2,1,0:T(8,128)S(1)}, f32[2,16,1]{2,1,0:T(8,128)S(1)}, u32[]{:S(2)}, u32[]{:S(2)}) collective-permute-start(f32[2,16,1]{2,1,0:T(8,128)S(1)} %get-tuple-element.14), channel_id=1, source_target_pairs={{0,1},{1,2},{2,3},{3,4},{4,5},{5,6},{6,7},{8,9},{9,10},{10,11},{11... | collective-permute-start | bytes 392 | tf_op jit(solution)/shard_map/ppermute | solution.py:340
  32.7 5.4 %collective-permute-start.2 = (f32[2,16,1]{2,1,0:T(8,128)S(1)}, f32[2,16,1]{2,1,0:T(8,128)S(1)}, u32[]{:S(2)}, u32[]{:S(2)}) collective-permute-start(f32[2,16,1]{2,1,0:T(8,128)S(1)} %get-tuple-element.15), channel_id=1, source_target_pairs={{1,0},{2,1},{3,2},{4,3},{5,4},{6,5},{7,6},{9,8},{10,9},{11,10},{12... | collective-permute-start | bytes 392 | tf_op jit(solution)/shard_map/ppermute | solution.py:341
  35.3 0.7 copy-start.6
  36.0 6.5 %copy-start.2 = (f32[128,1,1024]{2,1,0:T(1,128)S(1)}, f32[128,1,1024]{2,1,0:T(1,128)}, u32[]{:S(2)}) copy-start(f32[128,1,1024]{2,1,0:T(1,128)} %param.11) | copy-start | bytes 1572868
  42.4 16.7 %copy-start.1 = (f32[2,16,8192]{2,1,0:T(8,128)S(1)}, f32[2,16,8192]{2,1,0:T(8,128)}, u32[]{:S(2)}) copy-start(f32[2,16,8192]{2,1,0:T(8,128)} %v_ref.5) | copy-start | bytes 3145732
  44.2 14.9 %copy-start.3 = (f32[8192]{0:T(1024)S(1)}, f32[8192]{0:T(1024)}, u32[]{:S(2)}) copy-start(f32[8192]{0:T(1024)} %param.7) | copy-start | bytes 98308
  44.2 25.8 %all-to-all-start.1 = ((f32[64,4,128]{2,1,0:T(4,128)}), f32[64,4,128]{2,1,0:T(4,128)S(1)}, u32[]{:S(2)}, u32[]{:S(2)}) async-start(f32[64,4,128]{2,1,0:T(4,128)} %bitcast.6), calls=%async_computation.1 | async-start | bytes 262144 | tf_op jit(solution)/shard_map/all_to_all | solution.py:364
  54.6 9.5 %collective-permute-start.3 = (f32[2,16,2]{2,1,0:T(8,128)S(1)}, f32[2,16,2]{2,1,0:T(8,128)S(1)}, u32[]{:S(2)}, u32[]{:S(2)}) collective-permute-start(f32[2,16,2]{2,1,0:T(8,128)S(1)} %get-tuple-element.18), channel_id=1, source_target_pairs={{0,256},{8,264},{16,272},{24,280},{32,288},{40,296},{48,304},{56,3... | collective-permute-start | bytes 776 | tf_op jit(solution)/shard_map/ppermute | solution.py:365
  87.3 15.0 %all-to-all-start.3 = ((f32[16,4,128]{2,1,0:T(4,128)}), f32[16,4,128]{2,1,0:T(4,128)S(1)}, u32[]{:S(2)}, u32[]{:S(2)}) async-start(f32[16,4,128]{2,1,0:T(4,128)} %broadcast_in_dim.15), calls=%async_computation.3 | async-start | bytes 65536 | tf_op jit(solution)/shard_map/all_to_all | solution.py:313

commit v4 on v3

--- a/solution.py
+++ b/solution.py
@@ -58,9 +58,13 @@
 
 
 def own_terms(pair_ref, k2):
-    half = pair_ref.shape[0]
+    half = pair_ref.shape[-1]
     slot = 2 * harm_index() + k2
-    harmonic = jnp.full((OCT, LANES), pair_ref[lax.rem(slot, half)], jnp.int32)
+    if len(pair_ref.shape) == 1:
+        harmonic = jnp.full((OCT, LANES), pair_ref[lax.rem(slot, half)], jnp.int32)
+    else:
+        pairs = jnp.broadcast_to(jnp.concatenate([pair_ref[...]] * 2, axis=1), (OCT, LANES))
+        harmonic = pick(pairs, jnp.full((OCT, LANES), lax.rem(slot, half), jnp.int32))
     imag = jnp.full((OCT, LANES), slot, jnp.int32) >= half
     theta = angle_of(harmonic, imag, 2 * half)
     coup = jnp.where(harmonic == 0, 0.0, jnp.where(imag, -1.0, 1.0) * jnp.sin(theta))
@@ -82,16 +86,24 @@
     lax.fori_loop(0, attach_ref.shape[0] // group, step, 0)
 
 
-def gather_kernel(attach_ref, v_ref, out_ref, head_ref, tail_ref, t_ref, g_ref):
+def gather_kernel(attach_hbm, v_hbm, out_ref, head_ref, tail_ref, attach_ref, v_ref, t_ref, g_ref, sems):
+    parts, width = sems.shape[0] - 1, v_ref.shape[2]
+    span = width // parts
+    copies = [
+        pltpu.make_async_copy(v_hbm.at[:, :, pl.ds(n * span, span)], v_ref.at[:, :, pl.ds(n * span, span)], sems.at[n])
+        for n in range(parts)
+    ]
+    table = pltpu.make_async_copy(attach_hbm, attach_ref, sems.at[parts])
+    for copy in copies[:1] + [table] + copies[1:]:
+        copy.start()
+    for n, copy in enumerate(copies):
+        copy.wait()
+        for i in range(n * span // LANES, (n + 1) * span // LANES):
+            here = slice(LANES * i, LANES * (i + 1))
+            t_ref[here, :] = jnp.concatenate([v_ref[k2, o, here] for k2, o in OCTETS], axis=0).T
     head_ref[...] = v_ref[:, :, :1]
-    tail_ref[...] = v_ref[:, :, v_ref.shape[2] - 1 :]
-
-    def step(i, carry):
-        here = pl.ds(pl.multiple_of(i * LANES, LANES), LANES)
-        t_ref[here, :] = jnp.concatenate([v_ref[k2, o, here] for k2, o in OCTETS], axis=0).T
-        return carry
-
-    lax.fori_loop(0, v_ref.shape[2] // LANES, step, 0, unroll=32)
+    tail_ref[...] = v_ref[:, :, width - 1 :]
+    table.wait()
     fetch(attach_ref, t_ref, g_ref)
     owners = out_ref.shape[0] // 4
     part = iota((owners, LANES), 1) // 32
@@ -103,16 +115,9 @@
         out_ref[pl.ds(m, owners, stride=4), :] = out
 
 
-def table_kernel(pair_ref, attach_ref, partner_ref, basis_ref, inv_ref):
-    tiles, rows = inv_ref.shape[1], attach_ref.shape[1]
-    attach = attach_ref[...]
-    r = iota((1, rows), 1)
-    in_tile = (iota((tiles, rows), 0) == (attach >> 7)).astype(jnp.float32).astype(jnp.bfloat16)
-    in_lane = iota((LANES, rows), 0) == (attach & (LANES - 1))
-    for n, value in enumerate(((r >> 7) + 1, r & (LANES - 1))):
-        weighted = jnp.where(in_lane, value.astype(jnp.float32), 0.0).astype(jnp.bfloat16)
-        inv_ref[n] = lax.dot_general(in_tile, weighted, NT, preferred_element_type=jnp.float32).astype(jnp.int32)
-
+def table_kernel(pair_ref, basis_ref, coup_ref):
+    for k2 in range(2):
+        coup_ref[k2] = own_terms(pair_ref, k2)[1]
     half = pair_ref.shape[1]
     slots = 2 * half
     pairs = jnp.broadcast_to(jnp.concatenate([pair_ref[...]] * 2, axis=1), (OCT, slots))
@@ -203,10 +208,9 @@
     cols_ref[:, rows:] = g_ref[:LANES, :].T
 
 
-def blade_kernel(live_ref, recv_ref, mistune_ref, basis_ref, low_ref, high_ref, out_ref, edge_ref):
-    edge_ref[:, :, 0:1] = low_ref[...]
-    edge_ref[:, :, 1:2] = high_ref[...]
-    me, live = harm_index(), live_ref[0]
+def blade_kernel(live_ref, recv_ref, mistune_ref, basis_ref, out_ref, zero_ref):
+    zero_ref[...] = jnp.zeros(zero_ref.shape, jnp.float32)
+    me, live = harm_index(), live_ref[...]
     owners = out_ref.shape[0] // 4
     blades = 2 * owners
     slab = [recv_ref[pl.ds(m, owners, stride=4), :] for m in range(4)]
@@ -241,16 +245,15 @@
         out_ref[pl.ds(j, owners, stride=4), :] = turned[owners * k2 : owners * (k2 + 1), LANES * vh : LANES * (vh + 1)]
 
 
-def cross_kernel(width, pair_ref, attach_ref, recv_ref, cols_ref, gram_ref, low_ref, high_ref, p_edge_ref, total_ref, back_ref):
+def cross_kernel(width, coup_ref, attach_ref, recv_ref, cols_ref, gram_ref, low_ref, high_ref, p_edge_ref, total_ref, back_ref):
     vecs, rows = gram_ref.shape[1], attach_ref.shape[1]
     chunks = rows // LANES
     tiles = [[swap_blocks(recv_ref[pl.ds(4 * OCT * c + j, OCT, stride=4), :]) for c in range(chunks)] for j in range(4)]
-    total = gram_ref[...]
     attach = attach_ref[...]
     at_first, at_last = attach == 0, attach == width - 1
     lane = iota((vecs, LANES), 1)
     for k2 in range(2):
-        coup = own_terms(pair_ref, k2)[1][0:1, 0:1]
+        coup = coup_ref[k2, 0:1, 0:1]
         both = []
         for j in (2 * k2, 2 * k2 + 1):
             for c in range(chunks):
@@ -265,12 +268,25 @@
         adj = cols_ref[vecs * (k2 + 2) : vecs * (k2 + 3), :] + jnp.concatenate([at_rows, jnp.zeros_like(outer)], axis=1)
         left = jnp.concatenate([cols_ref[vecs * k2 : vecs * (k2 + 1), :], adj + 0.5 * more], axis=0)
         term = dot_f32(left, more, NT)
-        twice = dot_f32(more, left[vecs:], NT)
-        total = total + term + jnp.concatenate([jnp.zeros_like(twice), twice], axis=0)
-    total_ref[...] = total
-
-
-def image_kernel(pair_ref, inv_ref, stiff_ref, v_ref, p_ref, low_ref, high_ref, p_edge_ref, back_ref, image_ref):
+        terms = term if k2 == 0 else terms + term
+    unit = (iota((vecs, vecs), 0) == iota((vecs, vecs), 1)).astype(jnp.float32)
+    twice = dot_f32(unit, terms[vecs:], NT)
+    total_ref[...] = gram_ref[...] + terms + jnp.concatenate([jnp.zeros_like(twice), twice], axis=0)
+
+
+def inverse(attach_ref, inv_ref):
+    tiles, rows = inv_ref.shape[1], attach_ref.shape[1]
+    attach = attach_ref[...]
+    r = iota((1, rows), 1)
+    in_tile = (iota((tiles, rows), 0) == (attach >> 7)).astype(jnp.float32).astype(jnp.bfloat16)
+    in_lane = iota((LANES, rows), 0) == (attach & (LANES - 1))
+    for n, value in enumerate(((r >> 7) + 1, r & (LANES - 1))):
+        weighted = jnp.where(in_lane, value.astype(jnp.float32), 0.0).astype(jnp.bfloat16)
+        inv_ref[n] = lax.dot_general(in_tile, weighted, NT, preferred_element_type=jnp.float32).astype(jnp.int32)
+
+
+def image_kernel(pair_ref, attach_ref, stiff_ref, v_ref, p_ref, low_ref, high_ref, p_edge_ref, back_ref, image_ref, inv_ref):
+    inverse(attach_ref, inv_ref)
     tiles, chunks = inv_ref.shape[1], back_ref.shape[0] // 4
     at = adjusted(pair_ref, stiff_ref, v_ref, p_ref, (low_ref, high_ref, p_edge_ref))
 
@@ -327,11 +343,21 @@
     edge = jax.ShapeDtypeStruct((slot_count, vecs, 1), jnp.float32)
     packed, head, tail = pl.pallas_call(
         gather_kernel,
-        out_shape=(packed_rows, edge, edge),
-        in_specs=[smem(), vmem()],
+        out_shape=(
+            packed_rows,
+            edge,
+            edge,
+        ),
+        in_specs=[pl.BlockSpec(memory_space=pltpu.HBM)] * 2,
         out_specs=(vmem(),) * 3,
-        scratch_shapes=[pltpu.VMEM((width, 2 * vecs), jnp.float32), pltpu.VMEM((rows, 2 * vecs), jnp.float32)],
-        compiler_params=params(16),
+        scratch_shapes=[
+            pltpu.SMEM(attach.shape, jnp.int32),
+            pltpu.VMEM(vectors.shape, jnp.float32),
+            pltpu.VMEM((width, 2 * vecs), jnp.float32),
+            pltpu.VMEM((rows, 2 * vecs), jnp.float32),
+            pltpu.SemaphoreType.DMA((9,)),
+        ],
+        compiler_params=params(62),
         cost_estimate=cost(5),
         name="gather",
     )(attach, vectors)
@@ -340,29 +366,29 @@
     low_edge = lax.ppermute(tail, GRP, [(i, i + 1) for i in range(ends)])
     high_edge = lax.ppermute(head, GRP, [(i + 1, i) for i in range(ends)])
 
-    basis, inv = pl.pallas_call(
+    basis, coup = pl.pallas_call(
         table_kernel,
         out_shape=(
             jax.ShapeDtypeStruct((blades, blades), jnp.float32),
-            jax.ShapeDtypeStruct((2, tiles, LANES), jnp.int32),
+            jax.ShapeDtypeStruct((2, OCT, LANES), jnp.float32),
         ),
-        in_specs=[vmem()] * 2 + [pl.BlockSpec(memory_space=pl.ANY)],
+        in_specs=[vmem()],
         out_specs=(vmem(),) * 2,
         compiler_params=params(8),
-        cost_estimate=cost(60),
+        cost_estimate=cost(1),
         name="tables",
-    )(pair_harm.reshape(1, -1), attach.reshape(1, -1), partner)
-    back, own_edge = pl.pallas_call(
+    )(pair_harm.reshape(1, -1))
+    back, zero = pl.pallas_call(
         blade_kernel,
         out_shape=(packed_rows, jax.ShapeDtypeStruct((slot_count, vecs, 2), jnp.float32)),
-        in_specs=[smem()] + [vmem()] * 5,
+        in_specs=[vmem()] * 4,
         out_specs=(vmem(),) * 2,
         compiler_params=params(16),
-        cost_estimate=cost(4),
+        cost_estimate=cost(1),
         name="blades",
-    )(live, recv.reshape(4 * harm_size, LANES), mistune.reshape(-1, LANES), basis, low_edge, high_edge)
+    )(live.reshape(1, 1), recv.reshape(4 * harm_size, LANES), mistune.reshape(-1, LANES), basis)
     back = lax.all_to_all(back.reshape(harm_size, 4, LANES), HARM, 0, 0)
-    partner_edge = lax.ppermute(own_edge, HARM, to_partner)
+    partner_edge = lax.ppermute(jnp.concatenate([low_edge, high_edge], axis=2) + zero, HARM, to_partner)
 
     stiff = stiffness.reshape(-1, LANES)
     gram, cols = pl.pallas_call(
@@ -384,22 +410,23 @@
             jax.ShapeDtypeStruct((2 * vecs, vecs), jnp.float32),
             jax.ShapeDtypeStruct((4 * rows // LANES, OCT, LANES), jnp.float32),
         ),
-        in_specs=[smem()] + [vmem()] * 7,
+        in_specs=[vmem()] * 8,
         out_specs=(vmem(),) * 2,
         compiler_params=params(8),
         cost_estimate=cost(1),
         name="cross",
-    )(pair_harm, attach.reshape(1, -1), back.reshape(4 * harm_size, LANES), cols, gram, low_edge, high_edge, partner_edge)
+    )(coup, attach.reshape(1, -1), back.reshape(4 * harm_size, LANES), cols, gram, low_edge, high_edge, partner_edge)
     total = spread_sum(gram.reshape(4, LANES), PLANE)
     image = pl.pallas_call(
         image_kernel,
         out_shape=block,
         in_specs=[smem()] + [vmem()] * 8,
         out_specs=vmem(),
+        scratch_shapes=[pltpu.VMEM((2, tiles, LANES), jnp.int32)],
         compiler_params=params(8),
         cost_estimate=cost(20),
         name="image",
-    )(pair_harm, inv, stiff, vectors, partner, low_edge, high_edge, partner_edge, back_tiles)
+    )(pair_harm, attach.reshape(1, -1), stiff, vectors, partner, low_edge, high_edge, partner_edge, back_tiles)
     total = spread_sum(total, ("z",))
     return (image, total.reshape(2, vecs, vecs))
 

time: 104 us -> 102 us (0.981)
  local copies, waits for them, and re-layouts: 3.97 us -> 2.11 us
    unnamed x14, local copies, waits for them, and re-layouts: 2.57 us -> 0.68 us
    all_to_all x1, waiting for transfers between devices: 4.35 us -> 6.03 us  [local(): recv = lax.all_to_all(packed.reshape(harm_size, 4, LANES), HARM, 0, 0)]
    ppermute x1, waiting for transfers between devices: 1.65 us -> 0.01 us  [local(): high_edge = lax.ppermute(head, GRP, [(i + 1, i) for i in range(ends)])]
  transfers between devices with their start and end apart: 7 -> 7, of which waited for: 4 -> 3; matrix products, arithmetic and copies ran while one was open for 0% -> 0% of each run, Pallas kernels for 15% -> 18%
where the time goes in v4:
time: 102 us; the launch traced here: 101 us
  starting transfers between devices  46.3 us (45%)
  Pallas kernels  18.8 us (18%)
  waiting for transfers between devices  17.2 us (17%)
  blocking collectives  15 us (15%)
  local copies, waits for them, and re-layouts  2.11 us (2%)
  between operations  1.47 us (1%)
    all_to_all x1, starting transfers between devices, local(): recv = lax.all_to_all(packed.reshape(harm_size, 4, LANES), HARM, 0, 0)  16.3 us
    all_to_all x1, blocking collectives, spread_sum(): lax.all_to_all(jnp.broadcast_to(part[None], (count,) + part.shape), axes,...  15 us
    all_to_all x1, starting transfers between devices, local(): back = lax.all_to_all(back.reshape(harm_size, 4, LANES), HARM, 0, 0)  9.43 us
    all_to_all x1, waiting for transfers between devices, local(): recv = lax.all_to_all(packed.reshape(harm_size, 4, LANES), HARM, 0, 0)  6.03 us
    pallas_call x1, Pallas kernels, local(): pl.pallas_call(image_kernel, out_shape=block, in_specs=[smem()] + [vmem()...  6.03 us
    all_to_all x1, waiting for transfers between devices, local(): back = lax.all_to_all(back.reshape(harm_size, 4, LANES), HARM, 0, 0)  5.67 us
    ppermute x1, starting transfers between devices, local(): partner = lax.ppermute(vectors, HARM, to_partner)  5.65 us
    all_to_all x1, waiting for transfers between devices, spread_sum(): lax.all_to_all(jnp.broadcast_to(part[None], (count,) + part.shape), axes,...  5.44 us
  transfers between devices with their start and end apart: 7, of which 3 were waited for; matrix products, arithmetic and copies ran while one was open for 0% of the time, Pallas kernels for 18%

profile of v4, /device:TPU:1, one launch (start us, length us, event | category | flops | bytes accessed | tf_op | source)
XLA Modules:
  0.0 101.0 jit_solution(16619384217617232301)
XLA Ops:
  0.6 5.7 %collective-permute-start = (f32[2,16,8192]{2,1,0:T(8,128)}, f32[2,16,8192]{2,1,0:T(8,128)S(1)}, u32[]{:S(2)}, u32[]{:S(2)}) collective-permute-start(f32[2,16,8192]{2,1,0:T(8,128)} %v_ref.3), channel_id=1, source_target_pairs={{0,256},{8,264},{16,272},{24,280},{32,288},{40,296},{48,304},{56,3... | collective-permute-start | bytes 3145736 | tf_op jit(solution)/shard_map/ppermute | solution.py:342
  6.3 4.7 %gather.1 = (f32[256,128]{1,0:T(8,128)}, f32[2,16,1]{2,1,0:T(8,128)}, f32[2,16,1]{2,1,0:T(8,128)}) custom-call(s32[1024]{0:T(1024)} %attach_ref.1, f32[2,16,8192]{2,1,0:T(8,128)} %v_ref.3), custom_call_target="tpu_custom_call" | custom-call | flops 5000000000 | tf_op jit(solution)/shard_map/gather/pallas_call | solution.py:344
  11.0 0.0 copy-start.6
  11.0 0.0 copy-start.5
  11.0 16.3 %all-to-all-start = ((f32[64,4,128]{2,1,0:T(4,128)}), f32[64,4,128]{2,1,0:T(4,128)S(1)}, u32[]{:S(2)}, u32[]{:S(2)}) async-start(f32[64,4,128]{2,1,0:T(4,128)} %bitcast.18), calls=%async_computation | async-start | bytes 262144 | tf_op jit(solution)/shard_map/all_to_all | solution.py:364
  27.4 0.0 copy-done.6
  27.4 4.2 %collective-permute-start.1 = (f32[2,16,1]{2,1,0:T(8,128)S(1)}, f32[2,16,1]{2,1,0:T(8,128)S(1)}, u32[]{:S(2)}, u32[]{:S(2)}) collective-permute-start(f32[2,16,1]{2,1,0:T(8,128)S(1)} %copy-done.6), channel_id=1, source_target_pairs={{0,1},{1,2},{2,3},{3,4},{4,5},{5,6},{6,7},{8,9},{9,10},{10,11},{11... | collective-permute-start | bytes 392 | tf_op jit(solution)/shard_map/ppermute | solution.py:366
  31.6 0.0 copy-done.5
  31.6 1.9 %collective-permute-start.2 = (f32[2,16,1]{2,1,0:T(8,128)S(1)}, f32[2,16,1]{2,1,0:T(8,128)S(1)}, u32[]{:S(2)}, u32[]{:S(2)}) collective-permute-start(f32[2,16,1]{2,1,0:T(8,128)S(1)} %copy-done.5), channel_id=1, source_target_pairs={{1,0},{2,1},{3,2},{4,3},{5,4},{6,5},{7,6},{9,8},{10,9},{11,10},{12... | collective-permute-start | bytes 392 | tf_op jit(solution)/shard_map/ppermute | solution.py:367
  34.2 0.0 copy-start.4
  34.2 0.6 copy-done.4
  34.9 0.0 copy-start.1
  34.9 0.4 tables.1
  35.3 6.0 %all-to-all-done = f32[64,4,128]{2,1,0:T(4,128)S(1)} async-done(((f32[64,4,128]{2,1,0:T(4,128)}), f32[64,4,128]{2,1,0:T(4,128)S(1)}, u32[]{:S(2)}, u32[]{:S(2)}) %all-to-all-start) | async-done | bytes 131104 | tf_op jit(solution)/shard_map/all_to_all | solution.py:364
  41.3 0.0 copy-done.1
  41.3 0.0 copy-start
  41.3 1.8 %blades.1 = (f32[256,128]{1,0:T(8,128)}, f32[2,16,2]{2,1,0:T(8,128)S(1)}) custom-call(s32[1,1]{1,0:T(1,128)} %bitcast.9.live_ref, f32[256,128]{1,0:T(8,128)S(1)} %bitcast.11, f32[1024,128]{1,0:T(8,128)S(1)} %bitcast.12, f32[128,128]{1,0:T(8,128)S(1)} %get-tuple-element.16.basis_ref), custom_call_target="tpu_custom_call" | custom-call | flops 1000000000 | tf_op jit(solution)/shard_map/blades/pallas_call | solution.py:381
  43.1 9.4 %all-to-all-start.1 = ((f32[64,4,128]{2,1,0:T(4,128)}), f32[64,4,128]{2,1,0:T(4,128)S(1)}, u32[]{:S(2)}, u32[]{:S(2)}) async-start(f32[64,4,128]{2,1,0:T(4,128)} %bitcast.7), calls=%async_computation.1 | async-start | bytes 262144 | tf_op jit(solution)/shard_map/all_to_all | solution.py:390
  52.6 0.0 collective-permute-done.1.low_ref
  52.6 0.0 collective-permute-done.2.high_ref
  52.6 0.0 copy-start.2
  52.6 0.0 copy-start.3
  52.6 0.1 maximum_add_fusion
  52.7 4.5 %collective-permute-start.3 = (f32[2,16,2]{2,1,0:T(8,128)S(1)}, f32[2,16,2]{2,1,0:T(8,128)S(1)}, u32[]{:S(2)}, u32[]{:S(2)}) collective-permute-start(f32[2,16,2]{2,1,0:T(8,128)S(1)} %maximum_add_fusion), channel_id=1, source_target_pairs={{0,256},{8,264},{16,272},{24,280},{32,288},{40,296},{48,304},{56,3... | collective-permute-start | bytes 776 | tf_op jit(solution)/shard_map/ppermute | solution.py:391
  57.2 0.0 collective-permute-done.p_ref
  57.2 0.0 copy-done
  57.2 0.0 copy-done.2
  57.3 0.0 copy-done.3
  57.3 5.0 %adjust.1 = (f32[32,16]{1,0:T(8,128)S(1)}, f32[64,1152]{1,0:T(8,128)S(1)}) custom-call(s32[64]{0:T(128)S(1)} %copy-done.4, s32[1024]{0:T(1024)S(1)} %copy-done.3, f32[64,128]{1,0:T(8,128)S(1)} %bitcast.13, f32[2,16,8192]{2,1,0:T(8,128)S(1)} %copy-done, f32[2,16,8192]{2,1,0:T(8,128)S(1)} %collective-permute-done.p_ref), custom_call_target="tpu_custom_call" | custom-call | flops 40000000000 | tf_op jit(solution)/shard_map/adjust/pallas_call | solution.py:394
  62.2 0.0 collective-permute-done.3.p_edge_ref
  62.2 5.7 %all-to-all-done.1 = f32[64,4,128]{2,1,0:T(4,128)S(1)} async-done(((f32[64,4,128]{2,1,0:T(4,128)}), f32[64,4,128]{2,1,0:T(4,128)S(1)}, u32[]{:S(2)}, u32[]{:S(2)}) %all-to-all-start.1) | async-done | bytes 131104 | tf_op jit(solution)/shard_map/all_to_all | solution.py:390
  67.9 0.9 cross.1
  68.8 0.1 broadcast_in_dim.6
  68.9 15.0 %all_to_all.20 = f32[32,4,128]{2,1,0:T(4,128)S(1)} all-to-all(f32[32,4,128]{2,1,0:T(4,128)S(1)} %broadcast_in_dim.14), channel_id=1, replica_groups=mesh['y'=4,'z'=16,'x'=4,'core'=2] {'y','x','core'}, dimensions={0} | all-to-all | bytes 131072 | tf_op jit(solution)/shard_map/all_to_all | solution.py:329
  84.0 0.6 broadcast_in_dim.15
  84.6 4.2 %all-to-all-start.3 = ((f32[16,4,128]{2,1,0:T(4,128)}), f32[16,4,128]{2,1,0:T(4,128)S(1)}, u32[]{:S(2)}, u32[]{:S(2)}) async-start(f32[16,4,128]{2,1,0:T(4,128)} %broadcast_in_dim.15), calls=%async_computation.3 | async-start | bytes 65536 | tf_op jit(solution)/shard_map/all_to_all | solution.py:329
  88.8 6.0 %image.1 = f32[2,16,8192]{2,1,0:T(8,128)} custom-call(s32[64]{0:T(128)S(1)} %copy-done.4, s32[1,1024]{1,0:T(1,128)S(1)} %bitcast.16, f32[64,128]{1,0:T(8,128)S(1)} %bitcast.14, f32[2,16,8192]{2,1,0:T(8,128)S(1)} %copy-done, f32[2,16,8192]{2,1,0:T(8,128)S(1)} %collective-permute-done.p_ref, f32[2,16,1]{2,1,0:T(8,128)S(1)} %collective-permute-done.1.low_ref, ...), custom_call_target="tpu_custom_call" | custom-call | flops 20000000000 | tf_op jit(solution)/shard_map/image/pallas_call | solution.py:420
  94.8 5.4 %all-to-all-done.3 = f32[16,4,128]{2,1,0:T(4,128)S(1)} async-done(((f32[16,4,128]{2,1,0:T(4,128)}), f32[16,4,128]{2,1,0:T(4,128)S(1)}, u32[]{:S(2)}, u32[]{:S(2)}) %all-to-all-start.3) | async-done | bytes 32800 | tf_op jit(solution)/shard_map/all_to_all | solution.py:329
  100.3 0.7 reshape.46
  (3 shorter events, 0.1 us)
Async XLA Ops:
  0.6 56.6 %collective-permute-start = (f32[2,16,8192]{2,1,0:T(8,128)}, f32[2,16,8192]{2,1,0:T(8,128)S(1)}, u32[]{:S(2)}, u32[]{:S(2)}) collective-permute-start(f32[2,16,8192]{2,1,0:T(8,128)} %v_ref.3), channel_id=1, source_target_pairs={{0,256},{8,264},{16,272},{24,280},{32,288},{40,296},{48,304},{56,3... | collective-permute-start | bytes 3145736 | tf_op jit(solution)/shard_map/ppermute | solution.py:342
  11.0 16.4 %copy-start.6 = (f32[2,16,1]{2,1,0:T(8,128)S(1)}, f32[2,16,1]{2,1,0:T(8,128)}, u32[]{:S(2)}) copy-start(f32[2,16,1]{2,1,0:T(8,128)} %get-tuple-element.13) | copy-start | bytes 388
  11.0 20.6 %copy-start.5 = (f32[2,16,1]{2,1,0:T(8,128)S(1)}, f32[2,16,1]{2,1,0:T(8,128)}, u32[]{:S(2)}) copy-start(f32[2,16,1]{2,1,0:T(8,128)} %get-tuple-element.14) | copy-start | bytes 388
  11.0 30.3 %all-to-all-start = ((f32[64,4,128]{2,1,0:T(4,128)}), f32[64,4,128]{2,1,0:T(4,128)S(1)}, u32[]{:S(2)}, u32[]{:S(2)}) async-start(f32[64,4,128]{2,1,0:T(4,128)} %bitcast.18), calls=%async_computation | async-start | bytes 262144 | tf_op jit(solution)/shard_map/all_to_all | solution.py:364
  27.4 25.2 %collective-permute-start.1 = (f32[2,16,1]{2,1,0:T(8,128)S(1)}, f32[2,16,1]{2,1,0:T(8,128)S(1)}, u32[]{:S(2)}, u32[]{:S(2)}) collective-permute-start(f32[2,16,1]{2,1,0:T(8,128)S(1)} %copy-done.6), channel_id=1, source_target_pairs={{0,1},{1,2},{2,3},{3,4},{4,5},{5,6},{6,7},{8,9},{9,10},{10,11},{11... | collective-permute-start | bytes 392 | tf_op jit(solution)/shard_map/ppermute | solution.py:366
  31.6 21.0 %collective-permute-start.2 = (f32[2,16,1]{2,1,0:T(8,128)S(1)}, f32[2,16,1]{2,1,0:T(8,128)S(1)}, u32[]{:S(2)}, u32[]{:S(2)}) collective-permute-start(f32[2,16,1]{2,1,0:T(8,128)S(1)} %copy-done.5), channel_id=1, source_target_pairs={{1,0},{2,1},{3,2},{4,3},{5,4},{6,5},{7,6},{9,8},{10,9},{11,10},{12... | collective-permute-start | bytes 392 | tf_op jit(solution)/shard_map/ppermute | solution.py:367
  34.2 0.7 copy-start.4
  34.9 6.5 %copy-start.1 = (f32[128,1,1024]{2,1,0:T(1,128)S(1)}, f32[128,1,1024]{2,1,0:T(1,128)}, u32[]{:S(2)}) copy-start(f32[128,1,1024]{2,1,0:T(1,128)} %param.11) | copy-start | bytes 1572868
  41.3 15.9 %copy-start = (f32[2,16,8192]{2,1,0:T(8,128)S(1)}, f32[2,16,8192]{2,1,0:T(8,128)}, u32[]{:S(2)}) copy-start(f32[2,16,8192]{2,1,0:T(8,128)} %v_ref.3) | copy-start | bytes 3145732
  43.1 24.8 %all-to-all-start.1 = ((f32[64,4,128]{2,1,0:T(4,128)}), f32[64,4,128]{2,1,0:T(4,128)S(1)}, u32[]{:S(2)}, u32[]{:S(2)}) async-start(f32[64,4,128]{2,1,0:T(4,128)} %bitcast.7), calls=%async_computation.1 | async-start | bytes 262144 | tf_op jit(solution)/shard_map/all_to_all | solution.py:390
  52.6 4.6 %copy-start.2 = (f32[8192]{0:T(1024)S(1)}, f32[8192]{0:T(1024)}, u32[]{:S(2)}) copy-start(f32[8192]{0:T(1024)} %param.7) | copy-start | bytes 98308
  52.6 4.6 %copy-start.3 = (s32[1024]{0:T(1024)S(1)}, s32[1024]{0:T(1024)}, u32[]{:S(2)}) copy-start(s32[1024]{0:T(1024)} %attach_ref.1) | copy-start | bytes 12292
  52.7 9.5 %collective-permute-start.3 = (f32[2,16,2]{2,1,0:T(8,128)S(1)}, f32[2,16,2]{2,1,0:T(8,128)S(1)}, u32[]{:S(2)}, u32[]{:S(2)}) collective-permute-start(f32[2,16,2]{2,1,0:T(8,128)S(1)} %maximum_add_fusion), channel_id=1, source_target_pairs={{0,256},{8,264},{16,272},{24,280},{32,288},{40,296},{48,304},{56,3... | collective-permute-start | bytes 776 | tf_op jit(solution)/shard_map/ppermute | solution.py:391
  84.6 15.7 %all-to-all-start.3 = ((f32[16,4,128]{2,1,0:T(4,128)}), f32[16,4,128]{2,1,0:T(4,128)S(1)}, u32[]{:S(2)}, u32[]{:S(2)}) async-start(f32[16,4,128]{2,1,0:T(4,128)} %broadcast_in_dim.15), calls=%async_computation.3 | async-start | bytes 65536 | tf_op jit(solution)/shard_map/all_to_all | solution.py:329

commit v5 on v4

--- a/solution.py
+++ b/solution.py
@@ -208,10 +208,9 @@
     cols_ref[:, rows:] = g_ref[:LANES, :].T
 
 
-def blade_kernel(live_ref, recv_ref, mistune_ref, basis_ref, out_ref, zero_ref):
-    zero_ref[...] = jnp.zeros(zero_ref.shape, jnp.float32)
+def blade_kernel(live_ref, recv_ref, mistune_ref, basis_ref, low_ref, high_ref, out_ref):
     me, live = harm_index(), live_ref[...]
-    owners = out_ref.shape[0] // 4
+    owners = out_ref.shape[0] // 5
     blades = 2 * owners
     slab = [recv_ref[pl.ds(m, owners, stride=4), :] for m in range(4)]
     piece = iota((owners, LANES), 1) // PIECE
@@ -242,13 +241,26 @@
     turned = dot_f32(back, swap.astype(jnp.float32), mm)
     for j in range(4):
         k2, vh = j // 2, j % 2
-        out_ref[pl.ds(j, owners, stride=4), :] = turned[owners * k2 : owners * (k2 + 1), LANES * vh : LANES * (vh + 1)]
-
-
-def cross_kernel(width, coup_ref, attach_ref, recv_ref, cols_ref, gram_ref, low_ref, high_ref, p_edge_ref, total_ref, back_ref):
+        out_ref[pl.ds(j, owners, stride=5), :] = turned[owners * k2 : owners * (k2 + 1), LANES * vh : LANES * (vh + 1)]
+    column = jnp.concatenate([ref[k2] for ref in (low_ref, high_ref) for k2 in range(2)], axis=0)
+    shape = (column.shape[0], LANES)
+    row = jnp.sum(jnp.where(iota(shape, 0) == iota(shape, 1), column, 0.0), axis=0, keepdims=True)
+    out_ref[pl.ds(4, owners, stride=5), :] = jnp.broadcast_to(row, (owners, LANES))
+
+
+def cross_kernel(width, coup_ref, attach_ref, recv_ref, cols_ref, gram_ref, low_ref, high_ref, total_ref, back_ref, p_edge_ref):
     vecs, rows = gram_ref.shape[1], attach_ref.shape[1]
     chunks = rows // LANES
-    tiles = [[swap_blocks(recv_ref[pl.ds(4 * OCT * c + j, OCT, stride=4), :]) for c in range(chunks)] for j in range(4)]
+    tiles = [[swap_blocks(recv_ref[pl.ds(5 * OCT * c + j, OCT, stride=5), :]) for c in range(chunks)] for j in range(4)]
+    owners, me = recv_ref.shape[0] // 5, harm_index()
+    half = owners // 2
+    partner = jnp.where(me < half, me + half, me - half)
+    shape = (4 * vecs, LANES)
+    row = jnp.broadcast_to(recv_ref[pl.ds(5 * partner + 4, 1), :], shape)
+    outside = jnp.sum(jnp.where(iota(shape, 0) == iota(shape, 1), row, 0.0), axis=1, keepdims=True)
+    for n in range(2):
+        for k2 in range(2):
+            p_edge_ref[k2, :, n : n + 1] = outside[vecs * (2 * n + k2) : vecs * (2 * n + k2 + 1)]
     attach = attach_ref[...]
     at_first, at_last = attach == 0, attach == width - 1
     lane = iota((vecs, LANES), 1)
@@ -260,8 +272,8 @@
                 back_ref[4 * c + j] = tiles[j][c]
             both.append(jnp.concatenate(tiles[j], axis=1))
         back = jnp.concatenate(both, axis=0)
-        first = -low_ref[k2] - coup * p_edge_ref[k2, :, 0:1]
-        last = -high_ref[k2] + coup * p_edge_ref[k2, :, 1:2]
+        first = -low_ref[k2] - coup * outside[vecs * k2 : vecs * (k2 + 1)]
+        last = -high_ref[k2] + coup * outside[vecs * (k2 + 2) : vecs * (k2 + 3)]
         outer = jnp.where(lane == 0, first, jnp.where(lane == 1, last, 0.0))
         at_rows = jnp.where(at_first, first, jnp.where(at_last, last, 0.0))
         more = jnp.concatenate([back, outer], axis=1)
@@ -378,17 +390,17 @@
         cost_estimate=cost(1),
         name="tables",
     )(pair_harm.reshape(1, -1))
-    back, zero = pl.pallas_call(
+    carried = 5 * harm_size
+    back = pl.pallas_call(
         blade_kernel,
-        out_shape=(packed_rows, jax.ShapeDtypeStruct((slot_count, vecs, 2), jnp.float32)),
-        in_specs=[vmem()] * 4,
-        out_specs=(vmem(),) * 2,
+        out_shape=jax.ShapeDtypeStruct((carried, LANES), jnp.float32),
+        in_specs=[vmem()] * 6,
+        out_specs=vmem(),
         compiler_params=params(16),
         cost_estimate=cost(1),
         name="blades",
-    )(live.reshape(1, 1), recv.reshape(4 * harm_size, LANES), mistune.reshape(-1, LANES), basis)
-    back = lax.all_to_all(back.reshape(harm_size, 4, LANES), HARM, 0, 0)
-    partner_edge = lax.ppermute(jnp.concatenate([low_edge, high_edge], axis=2) + zero, HARM, to_partner)
+    )(live.reshape(1, 1), recv.reshape(4 * harm_size, LANES), mistune.reshape(-1, LANES), basis, low_edge, high_edge)
+    back = lax.all_to_all(back.reshape(carried, 1, LANES), HARM, 0, 0, tiled=True).reshape(carried, LANES)
 
     stiff = stiffness.reshape(-1, LANES)
     gram, cols = pl.pallas_call(
@@ -404,18 +416,19 @@
         cost_estimate=cost(40),
         name="adjust",
     )(pair_harm, attach, stiff, vectors, partner)
-    gram, back_tiles = pl.pallas_call(
+    gram, back_tiles, partner_edge = pl.pallas_call(
         functools.partial(cross_kernel, width),
         out_shape=(
             jax.ShapeDtypeStruct((2 * vecs, vecs), jnp.float32),
             jax.ShapeDtypeStruct((4 * rows // LANES, OCT, LANES), jnp.float32),
+            jax.ShapeDtypeStruct((slot_count, vecs, 2), jnp.float32),
         ),
-        in_specs=[vmem()] * 8,
-        out_specs=(vmem(),) * 2,
+        in_specs=[vmem()] * 7,
+        out_specs=(vmem(),) * 3,
         compiler_params=params(8),
         cost_estimate=cost(1),
         name="cross",
-    )(coup, attach.reshape(1, -1), back.reshape(4 * harm_size, LANES), cols, gram, low_edge, high_edge, partner_edge)
+    )(coup, attach.reshape(1, -1), back, cols, gram, low_edge, high_edge)
     total = spread_sum(gram.reshape(4, LANES), PLANE)
     image = pl.pallas_call(
         image_kernel,

time: 102 us -> 103 us (level)
  waiting for transfers between devices: 17.2 us -> 24 us
  starting transfers between devices: 46.3 us -> 42 us
    all_to_all x1, waiting for transfers between devices: 5.67 us -> 11.9 us  [local(): lax.all_to_all(back.reshape(carried, 1, LANES), HARM, 0, 0, tiled=True)]
    ppermute x1 -> x0, starting transfers between devices: 4.51 us -> none  [local(): lax.ppermute(jnp.concatenate([low_edge, high_edge], axis=2) + zero, HARM,...]
    ppermute x1, waiting for transfers between devices: 0.01 us -> 2.31 us  [local(): high_edge = lax.ppermute(head, GRP, [(i + 1, i) for i in range(ends)])]
    all_to_all x1, waiting for transfers between devices: 6.03 us -> 4.33 us  [local(): recv = lax.all_to_all(packed.reshape(harm_size, 4, LANES), HARM, 0, 0)]
  transfers between devices with their start and end apart: 7 -> 6, of which waited for: 3 -> 4; matrix products, arithmetic and copies ran while one was open for 0% -> 0% of each run, Pallas kernels for 18% -> 18%
where the time goes in v5:
time: 103 us; the launch traced here: 102 us
  starting transfers between devices  42 us (41%)
  waiting for transfers between devices  24 us (23%)
  Pallas kernels  18.8 us (18%)
  blocking collectives  14.4 us (14%)
  local copies, waits for them, and re-layouts  1.47 us (1%)
  between operations  1.45 us (1%)
    all_to_all x1, starting transfers between devices, local(): recv = lax.all_to_all(packed.reshape(harm_size, 4, LANES), HARM, 0, 0)  16.3 us
    all_to_all x1, blocking collectives, spread_sum(): lax.all_to_all(jnp.broadcast_to(part[None], (count,) + part.shape), axes,...  14.4 us
    all_to_all x1, waiting for transfers between devices, local(): lax.all_to_all(back.reshape(carried, 1, LANES), HARM, 0, 0, tiled=True)  11.9 us
    all_to_all x1, starting transfers between devices, local(): lax.all_to_all(back.reshape(carried, 1, LANES), HARM, 0, 0, tiled=True)  10.4 us
    pallas_call x1, Pallas kernels, local(): pl.pallas_call(image_kernel, out_shape=block, in_specs=[smem()] + [vmem()...  6.03 us
    ppermute x1, starting transfers between devices, local(): partner = lax.ppermute(vectors, HARM, to_partner)  5.65 us
    all_to_all x1, waiting for transfers between devices, spread_sum(): lax.all_to_all(jnp.broadcast_to(part[None], (count,) + part.shape), axes,...  5.44 us
    pallas_call x1, Pallas kernels, local(): pl.pallas_call(adjust_kernel, out_shape=(jax.ShapeDtypeStruct((2 * vecs,...  4.97 us
  transfers between devices with their start and end apart: 6, of which 4 were waited for; matrix products, arithmetic and copies ran while one was open for 0% of the time, Pallas kernels for 18%

profile of v5, /device:TPU:1, one launch (start us, length us, event | category | flops | bytes accessed | tf_op | source)
XLA Modules:
  0.0 102.2 jit_solution(16902881142280951725)
XLA Ops:
  0.6 5.7 %collective-permute-start = (f32[2,16,8192]{2,1,0:T(8,128)}, f32[2,16,8192]{2,1,0:T(8,128)S(1)}, u32[]{:S(2)}, u32[]{:S(2)}) collective-permute-start(f32[2,16,8192]{2,1,0:T(8,128)} %v_ref.3), channel_id=1, source_target_pairs={{0,256},{8,264},{16,272},{24,280},{32,288},{40,296},{48,304},{56,3... | collective-permute-start | bytes 3145736 | tf_op jit(solution)/shard_map/ppermute | solution.py:354
  6.3 4.7 %gather.1 = (f32[256,128]{1,0:T(8,128)}, f32[2,16,1]{2,1,0:T(8,128)}, f32[2,16,1]{2,1,0:T(8,128)}) custom-call(s32[1024]{0:T(1024)} %attach_ref.1, f32[2,16,8192]{2,1,0:T(8,128)} %v_ref.3), custom_call_target="tpu_custom_call" | custom-call | flops 5000000000 | tf_op jit(solution)/shard_map/gather/pallas_call | solution.py:356
  11.0 0.0 copy-start.6
  11.0 0.0 copy-start.5
  11.0 16.3 %all-to-all-start = ((f32[64,4,128]{2,1,0:T(4,128)}), f32[64,4,128]{2,1,0:T(4,128)S(1)}, u32[]{:S(2)}, u32[]{:S(2)}) async-start(f32[64,4,128]{2,1,0:T(4,128)} %bitcast.20), calls=%async_computation | async-start | bytes 262144 | tf_op jit(solution)/shard_map/all_to_all | solution.py:376
  27.4 0.0 copy-done.6
  27.4 4.2 %collective-permute-start.1 = (f32[2,16,1]{2,1,0:T(8,128)S(1)}, f32[2,16,1]{2,1,0:T(8,128)S(1)}, u32[]{:S(2)}, u32[]{:S(2)}) collective-permute-start(f32[2,16,1]{2,1,0:T(8,128)S(1)} %copy-done.6), channel_id=1, source_target_pairs={{0,1},{1,2},{2,3},{3,4},{4,5},{5,6},{6,7},{8,9},{9,10},{10,11},{11... | collective-permute-start | bytes 392 | tf_op jit(solution)/shard_map/ppermute | solution.py:378
  31.6 0.0 copy-done.5
  31.6 0.0 copy-start.4
  31.6 1.9 %collective-permute-start.2 = (f32[2,16,1]{2,1,0:T(8,128)S(1)}, f32[2,16,1]{2,1,0:T(8,128)S(1)}, u32[]{:S(2)}, u32[]{:S(2)}) collective-permute-start(f32[2,16,1]{2,1,0:T(8,128)S(1)} %copy-done.5), channel_id=1, source_target_pairs={{1,0},{2,1},{3,2},{4,3},{5,4},{6,5},{7,6},{9,8},{10,9},{11,10},{12... | collective-permute-start | bytes 392 | tf_op jit(solution)/shard_map/ppermute | solution.py:379
  33.6 0.0 copy-done.4
  33.6 0.0 copy-start.1
  33.6 0.4 tables.1
  34.7 0.0 collective-permute-done.1.low_ref
  34.7 2.3 %collective-permute-done.2.high_ref = f32[2,16,1]{2,1,0:T(8,128)S(1)} collective-permute-done((f32[2,16,1]{2,1,0:T(8,128)S(1)}, f32[2,16,1]{2,1,0:T(8,128)S(1)}, u32[]{:S(2)}, u32[]{:S(2)}) %collective-permute-start.2) | collective-permute-done | bytes 160 | tf_op jit(solution)/shard_map/ppermute | solution.py:379
  37.0 4.3 %all-to-all-done = f32[64,4,128]{2,1,0:T(4,128)S(1)} async-done(((f32[64,4,128]{2,1,0:T(4,128)}), f32[64,4,128]{2,1,0:T(4,128)S(1)}, u32[]{:S(2)}, u32[]{:S(2)}) %all-to-all-start) | async-done | bytes 131104 | tf_op jit(solution)/shard_map/all_to_all | solution.py:376
  41.3 0.0 copy-done.1
  41.3 0.0 copy-start
  41.3 1.8 %blades.1 = f32[320,128]{1,0:T(8,128)} custom-call(s32[1,1]{1,0:T(1,128)} %bitcast.11.live_ref, f32[256,128]{1,0:T(8,128)S(1)} %bitcast.13, f32[1024,128]{1,0:T(8,128)S(1)} %bitcast.14, f32[128,128]{1,0:T(8,128)S(1)} %get-tuple-element.16.basis_ref, f32[2,16,1]{2,1,0:T(8,128)S(1)} %collective-permute-done.1.low_ref, ...), custom_call_target="tpu_custom_call" | custom-call | flops 1000000000 | tf_op jit(solution)/shard_map/blades/pallas_call | solution.py:394
  43.2 0.0 copy-start.2
  43.2 0.0 copy-start.3
  43.2 10.4 %all-to-all-start.1 = ((f32[320,1,128]{2,1,0:T(1,128)}), f32[320,1,128]{2,1,0:T(1,128)S(1)}, u32[]{:S(2)}, u32[]{:S(2)}) async-start(f32[320,1,128]{2,1,0:T(1,128)} %bitcast.8), calls=%async_computation.1 | async-start | bytes 327680 | tf_op jit(solution)/shard_map/all_to_all | solution.py:403
  53.5 0.0 collective-permute-done.p_ref
  53.5 0.0 copy-done
  53.5 0.0 copy-done.2
  53.6 0.0 copy-done.3
  53.6 5.0 %adjust.1 = (f32[32,16]{1,0:T(8,128)S(1)}, f32[64,1152]{1,0:T(8,128)S(1)}) custom-call(s32[64]{0:T(128)S(1)} %copy-done.4, s32[1024]{0:T(1024)S(1)} %copy-done.3, f32[64,128]{1,0:T(8,128)S(1)} %bitcast.15, f32[2,16,8192]{2,1,0:T(8,128)S(1)} %copy-done, f32[2,16,8192]{2,1,0:T(8,128)S(1)} %collective-permute-done.p_ref), custom_call_target="tpu_custom_call" | custom-call | flops 40000000000 | tf_op jit(solution)/shard_map/adjust/pallas_call | solution.py:406
  58.5 11.9 %all-to-all-done.1 = f32[320,1,128]{2,1,0:T(1,128)S(1)} async-done(((f32[320,1,128]{2,1,0:T(1,128)}), f32[320,1,128]{2,1,0:T(1,128)S(1)}, u32[]{:S(2)}, u32[]{:S(2)}) %all-to-all-start.1) | async-done | bytes 163872 | tf_op jit(solution)/shard_map/all_to_all | solution.py:403
  70.5 0.9 cross.1
  71.3 0.1 broadcast_in_dim.6
  71.5 14.4 %all_to_all.20 = f32[32,4,128]{2,1,0:T(4,128)S(1)} all-to-all(f32[32,4,128]{2,1,0:T(4,128)S(1)} %broadcast_in_dim.14), channel_id=1, replica_groups=mesh['y'=4,'z'=16,'x'=4,'core'=2] {'y','x','core'}, dimensions={0} | all-to-all | bytes 131072 | tf_op jit(solution)/shard_map/all_to_all | solution.py:341
  85.9 0.6 broadcast_in_dim.15
  86.5 3.5 %all-to-all-start.3 = ((f32[16,4,128]{2,1,0:T(4,128)}), f32[16,4,128]{2,1,0:T(4,128)S(1)}, u32[]{:S(2)}, u32[]{:S(2)}) async-start(f32[16,4,128]{2,1,0:T(4,128)} %broadcast_in_dim.15), calls=%async_computation.3 | async-start | bytes 65536 | tf_op jit(solution)/shard_map/all_to_all | solution.py:341
  90.0 6.0 %image.1 = f32[2,16,8192]{2,1,0:T(8,128)} custom-call(s32[64]{0:T(128)S(1)} %copy-done.4, s32[1,1024]{1,0:T(1,128)S(1)} %bitcast.18, f32[64,128]{1,0:T(8,128)S(1)} %bitcast.16, f32[2,16,8192]{2,1,0:T(8,128)S(1)} %copy-done, f32[2,16,8192]{2,1,0:T(8,128)S(1)} %collective-permute-done.p_ref, f32[2,16,1]{2,1,0:T(8,128)S(1)} %collective-permute-done.1.low_ref, ...), custom_call_target="tpu_custom_call" | custom-call | flops 20000000000 | tf_op jit(solution)/shard_map/image/pallas_call | solution.py:433
  96.1 5.4 %all-to-all-done.3 = f32[16,4,128]{2,1,0:T(4,128)S(1)} async-done(((f32[16,4,128]{2,1,0:T(4,128)}), f32[16,4,128]{2,1,0:T(4,128)S(1)}, u32[]{:S(2)}, u32[]{:S(2)}) %all-to-all-start.3) | async-done | bytes 32800 | tf_op jit(solution)/shard_map/all_to_all | solution.py:341
  101.5 0.7 reshape.46
  (3 shorter events, 0.1 us)
Async XLA Ops:
  0.6 52.9 %collective-permute-start = (f32[2,16,8192]{2,1,0:T(8,128)}, f32[2,16,8192]{2,1,0:T(8,128)S(1)}, u32[]{:S(2)}, u32[]{:S(2)}) collective-permute-start(f32[2,16,8192]{2,1,0:T(8,128)} %v_ref.3), channel_id=1, source_target_pairs={{0,256},{8,264},{16,272},{24,280},{32,288},{40,296},{48,304},{56,3... | collective-permute-start | bytes 3145736 | tf_op jit(solution)/shard_map/ppermute | solution.py:354
  11.0 16.4 %copy-start.6 = (f32[2,16,1]{2,1,0:T(8,128)S(1)}, f32[2,16,1]{2,1,0:T(8,128)}, u32[]{:S(2)}) copy-start(f32[2,16,1]{2,1,0:T(8,128)} %get-tuple-element.12) | copy-start | bytes 388
  11.0 20.6 %copy-start.5 = (f32[2,16,1]{2,1,0:T(8,128)S(1)}, f32[2,16,1]{2,1,0:T(8,128)}, u32[]{:S(2)}) copy-start(f32[2,16,1]{2,1,0:T(8,128)} %get-tuple-element.13) | copy-start | bytes 388
  11.0 30.3 %all-to-all-start = ((f32[64,4,128]{2,1,0:T(4,128)}), f32[64,4,128]{2,1,0:T(4,128)S(1)}, u32[]{:S(2)}, u32[]{:S(2)}) async-start(f32[64,4,128]{2,1,0:T(4,128)} %bitcast.20), calls=%async_computation | async-start | bytes 262144 | tf_op jit(solution)/shard_map/all_to_all | solution.py:376
  27.4 7.3 %collective-permute-start.1 = (f32[2,16,1]{2,1,0:T(8,128)S(1)}, f32[2,16,1]{2,1,0:T(8,128)S(1)}, u32[]{:S(2)}, u32[]{:S(2)}) collective-permute-start(f32[2,16,1]{2,1,0:T(8,128)S(1)} %copy-done.6), channel_id=1, source_target_pairs={{0,1},{1,2},{2,3},{3,4},{4,5},{5,6},{6,7},{8,9},{9,10},{10,11},{11... | collective-permute-start | bytes 392 | tf_op jit(solution)/shard_map/ppermute | solution.py:378
  31.6 1.9 %copy-start.4 = (s32[64]{0:T(128)S(1)}, s32[64]{0:T(128)}, u32[]{:S(2)}) copy-start(s32[64]{0:T(128)} %pair_ref.3) | copy-start | bytes 772
  31.6 5.4 %collective-permute-start.2 = (f32[2,16,1]{2,1,0:T(8,128)S(1)}, f32[2,16,1]{2,1,0:T(8,128)S(1)}, u32[]{:S(2)}, u32[]{:S(2)}) collective-permute-start(f32[2,16,1]{2,1,0:T(8,128)S(1)} %copy-done.5), channel_id=1, source_target_pairs={{1,0},{2,1},{3,2},{4,3},{5,4},{6,5},{7,6},{9,8},{10,9},{11,10},{12... | collective-permute-start | bytes 392 | tf_op jit(solution)/shard_map/ppermute | solution.py:379
  33.6 7.7 %copy-start.1 = (f32[128,1,1024]{2,1,0:T(1,128)S(1)}, f32[128,1,1024]{2,1,0:T(1,128)}, u32[]{:S(2)}) copy-start(f32[128,1,1024]{2,1,0:T(1,128)} %param.11) | copy-start | bytes 1572868
  41.3 12.2 %copy-start = (f32[2,16,8192]{2,1,0:T(8,128)S(1)}, f32[2,16,8192]{2,1,0:T(8,128)}, u32[]{:S(2)}) copy-start(f32[2,16,8192]{2,1,0:T(8,128)} %v_ref.3) | copy-start | bytes 3145732
  43.2 10.4 %copy-start.2 = (f32[8192]{0:T(1024)S(1)}, f32[8192]{0:T(1024)}, u32[]{:S(2)}) copy-start(f32[8192]{0:T(1024)} %param.7) | copy-start | bytes 98308
  43.2 10.4 %copy-start.3 = (s32[1024]{0:T(1024)S(1)}, s32[1024]{0:T(1024)}, u32[]{:S(2)}) copy-start(s32[1024]{0:T(1024)} %attach_ref.1) | copy-start | bytes 12292
  43.2 27.3 %all-to-all-start.1 = ((f32[320,1,128]{2,1,0:T(1,128)}), f32[320,1,128]{2,1,0:T(1,128)S(1)}, u32[]{:S(2)}, u32[]{:S(2)}) async-start(f32[320,1,128]{2,1,0:T(1,128)} %bitcast.8), calls=%async_computation.1 | async-start | bytes 327680 | tf_op jit(solution)/shard_map/all_to_all | solution.py:403
  86.5 15.0 %all-to-all-start.3 = ((f32[16,4,128]{2,1,0:T(4,128)}), f32[16,4,128]{2,1,0:T(4,128)S(1)}, u32[]{:S(2)}, u32[]{:S(2)}) async-start(f32[16,4,128]{2,1,0:T(4,128)} %broadcast_in_dim.15), calls=%async_computation.3 | async-start | bytes 65536 | tf_op jit(solution)/shard_map/all_to_all | solution.py:341

commit v6 on v4

--- a/solution.py
+++ b/solution.py
@@ -115,7 +115,12 @@
         out_ref[pl.ds(m, owners, stride=4), :] = out
 
 
-def table_kernel(pair_ref, basis_ref, coup_ref):
+def table_kernel(pair_ref, mistune_ref, basis_ref, coup_ref, stiff_ref):
+    me, blades = harm_index(), basis_ref.shape[0]
+    chunk = mistune_ref[pl.ds(me // OCT, blades, stride=OCT), :]
+    index = lax.rem(me, OCT) * PIECE + iota((blades, LANES), 1) // PIECE
+    stiff_ref[:, :LANES] = pick(chunk, index)
+    stiff_ref[:, LANES:] = pick(chunk, index + OCT)
     for k2 in range(2):
         coup_ref[k2] = own_terms(pair_ref, k2)[1]
     half = pair_ref.shape[1]
@@ -208,7 +213,7 @@
     cols_ref[:, rows:] = g_ref[:LANES, :].T
 
 
-def blade_kernel(live_ref, recv_ref, mistune_ref, basis_ref, out_ref, zero_ref):
+def blade_kernel(live_ref, recv_ref, stiff_ref, basis_ref, out_ref, zero_ref):
     zero_ref[...] = jnp.zeros(zero_ref.shape, jnp.float32)
     me, live = harm_index(), live_ref[...]
     owners = out_ref.shape[0] // 4
@@ -233,13 +238,12 @@
     rows = jnp.where(alive, jnp.concatenate([arrived(0), arrived(1)], axis=0), 0.0)
     mm = (((1,), (0,)), ((), ()))
     blade = dot_f32(basis_ref[...], rows, mm)
-    chunk = mistune_ref[pl.ds(me // OCT, blades, stride=OCT), :]
-    index = lax.rem(me, OCT) * PIECE + iota((blades, LANES), 1) // PIECE
-    stiff = jnp.concatenate([pick(chunk, index), pick(chunk, index + OCT)], axis=1)
-    back = jnp.where(alive, dot_f32(basis_ref[...], stiff * blade, TN), 0.0)
+    back = jnp.where(alive, dot_f32(basis_ref[...], stiff_ref[...] * blade, TN), 0.0)
     down, across = iota((wide, wide), 0), iota((wide, wide), 1)
     swap = ((down & (PIECE - 1)) == across // PIECE) & (down // PIECE == (across & (PIECE - 1)))
-    turned = dot_f32(back, swap.astype(jnp.float32), mm)
+    parts = jnp.concatenate(split(back, 3), axis=0)
+    parts = jnp.dot(parts, swap.astype(jnp.float32).astype(jnp.bfloat16), preferred_element_type=jnp.float32)
+    turned = parts[:blades] + parts[blades : 2 * blades] + parts[2 * blades :]
     for j in range(4):
         k2, vh = j // 2, j % 2
         out_ref[pl.ds(j, owners, stride=4), :] = turned[owners * k2 : owners * (k2 + 1), LANES * vh : LANES * (vh + 1)]
@@ -366,18 +370,19 @@
     low_edge = lax.ppermute(tail, GRP, [(i, i + 1) for i in range(ends)])
     high_edge = lax.ppermute(head, GRP, [(i + 1, i) for i in range(ends)])
 
-    basis, coup = pl.pallas_call(
+    basis, coup, stiff_rows = pl.pallas_call(
         table_kernel,
         out_shape=(
             jax.ShapeDtypeStruct((blades, blades), jnp.float32),
             jax.ShapeDtypeStruct((2, OCT, LANES), jnp.float32),
+            jax.ShapeDtypeStruct((blades, 2 * LANES), jnp.float32),
         ),
-        in_specs=[vmem()],
-        out_specs=(vmem(),) * 2,
+        in_specs=[vmem()] * 2,
+        out_specs=(vmem(),) * 3,
         compiler_params=params(8),
         cost_estimate=cost(1),
         name="tables",
-    )(pair_harm.reshape(1, -1))
+    )(pair_harm.reshape(1, -1), mistune.reshape(-1, LANES))
     back, zero = pl.pallas_call(
         blade_kernel,
         out_shape=(packed_rows, jax.ShapeDtypeStruct((slot_count, vecs, 2), jnp.float32)),
@@ -386,7 +391,7 @@
         compiler_params=params(16),
         cost_estimate=cost(1),
         name="blades",
-    )(live.reshape(1, 1), recv.reshape(4 * harm_size, LANES), mistune.reshape(-1, LANES), basis)
+    )(live.reshape(1, 1), recv.reshape(4 * harm_size, LANES), stiff_rows, basis)
     back = lax.all_to_all(back.reshape(harm_size, 4, LANES), HARM, 0, 0)
     partner_edge = lax.ppermute(jnp.concatenate([low_edge, high_edge], axis=2) + zero, HARM, to_partner)
 

time: 102 us -> 101 us (level)
  no operation moved by 1% of the time
where the time goes in v6:
time: 101 us; the launch traced here: 100 us
  starting transfers between devices  45.8 us (45%)
  Pallas kernels  18.7 us (19%)
  waiting for transfers between devices  16.3 us (16%)
  blocking collectives  15.9 us (16%)
  local copies, waits for them, and re-layouts  2.1 us (2%)
  between operations  1.49 us (1%)
    all_to_all x1, starting transfers between devices, local(): recv = lax.all_to_all(packed.reshape(harm_size, 4, LANES), HARM, 0, 0)  16.3 us
    all_to_all x1, blocking collectives, spread_sum(): lax.all_to_all(jnp.broadcast_to(part[None], (count,) + part.shape), axes,...  15.9 us
    all_to_all x1, starting transfers between devices, local(): back = lax.all_to_all(back.reshape(harm_size, 4, LANES), HARM, 0, 0)  8.84 us
    all_to_all x1, waiting for transfers between devices, local(): recv = lax.all_to_all(packed.reshape(harm_size, 4, LANES), HARM, 0, 0)  6.03 us
    pallas_call x1, Pallas kernels, local(): pl.pallas_call(image_kernel, out_shape=block, in_specs=[smem()] + [vmem()...  6.03 us
    ppermute x1, starting transfers between devices, local(): partner = lax.ppermute(vectors, HARM, to_partner)  5.79 us
    all_to_all x1, waiting for transfers between devices, spread_sum(): lax.all_to_all(jnp.broadcast_to(part[None], (count,) + part.shape), axes,...  5.44 us
    pallas_call x1, Pallas kernels, local(): pl.pallas_call(adjust_kernel, out_shape=(jax.ShapeDtypeStruct((2 * vecs,...  4.97 us
  transfers between devices with their start and end apart: 7, of which 3 were waited for; matrix products, arithmetic and copies ran while one was open for 0% of the time, Pallas kernels for 18%

profile of v6, /device:TPU:1, one launch (start us, length us, event | category | flops | bytes accessed | tf_op | source)
XLA Modules:
  0.0 100.5 jit_solution(11552239448240402145)
XLA Ops:
  0.6 0.0 copy-start.1
  0.6 5.8 %collective-permute-start = (f32[2,16,8192]{2,1,0:T(8,128)}, f32[2,16,8192]{2,1,0:T(8,128)S(1)}, u32[]{:S(2)}, u32[]{:S(2)}) collective-permute-start(f32[2,16,8192]{2,1,0:T(8,128)} %v_ref.3), channel_id=1, source_target_pairs={{0,256},{8,264},{16,272},{24,280},{32,288},{40,296},{48,304},{56,3... | collective-permute-start | bytes 3145736 | tf_op jit(solution)/shard_map/ppermute | solution.py:346
  6.4 4.7 %gather.1 = (f32[256,128]{1,0:T(8,128)}, f32[2,16,1]{2,1,0:T(8,128)}, f32[2,16,1]{2,1,0:T(8,128)}) custom-call(s32[1024]{0:T(1024)} %attach_ref.1, f32[2,16,8192]{2,1,0:T(8,128)} %v_ref.3), custom_call_target="tpu_custom_call" | custom-call | flops 5000000000 | tf_op jit(solution)/shard_map/gather/pallas_call | solution.py:348
  11.1 0.0 copy-start.6
  11.2 0.0 copy-start.5
  11.2 16.3 %all-to-all-start = ((f32[64,4,128]{2,1,0:T(4,128)}), f32[64,4,128]{2,1,0:T(4,128)S(1)}, u32[]{:S(2)}, u32[]{:S(2)}) async-start(f32[64,4,128]{2,1,0:T(4,128)} %bitcast.18), calls=%async_computation | async-start | bytes 262144 | tf_op jit(solution)/shard_map/all_to_all | solution.py:368
  27.5 0.0 copy-done.6
  27.5 4.2 %collective-permute-start.1 = (f32[2,16,1]{2,1,0:T(8,128)S(1)}, f32[2,16,1]{2,1,0:T(8,128)S(1)}, u32[]{:S(2)}, u32[]{:S(2)}) collective-permute-start(f32[2,16,1]{2,1,0:T(8,128)S(1)} %copy-done.6), channel_id=1, source_target_pairs={{0,1},{1,2},{2,3},{3,4},{4,5},{5,6},{6,7},{8,9},{9,10},{10,11},{11... | collective-permute-start | bytes 392 | tf_op jit(solution)/shard_map/ppermute | solution.py:370
  31.8 0.0 copy-done.5
  31.8 1.9 %collective-permute-start.2 = (f32[2,16,1]{2,1,0:T(8,128)S(1)}, f32[2,16,1]{2,1,0:T(8,128)S(1)}, u32[]{:S(2)}, u32[]{:S(2)}) collective-permute-start(f32[2,16,1]{2,1,0:T(8,128)S(1)} %copy-done.5), channel_id=1, source_target_pairs={{1,0},{2,1},{3,2},{4,3},{5,4},{6,5},{7,6},{9,8},{10,9},{11,10},{12... | collective-permute-start | bytes 392 | tf_op jit(solution)/shard_map/ppermute | solution.py:371
  34.3 0.0 copy-start.4
  34.4 0.0 copy-done.1
  34.4 0.6 copy-done.4
  35.0 0.4 tables.1
  35.4 6.0 %all-to-all-done = f32[64,4,128]{2,1,0:T(4,128)S(1)} async-done(((f32[64,4,128]{2,1,0:T(4,128)}), f32[64,4,128]{2,1,0:T(4,128)S(1)}, u32[]{:S(2)}, u32[]{:S(2)}) %all-to-all-start) | async-done | bytes 131104 | tf_op jit(solution)/shard_map/all_to_all | solution.py:368
  41.5 0.0 copy-start
  41.5 1.8 %blades.1 = (f32[256,128]{1,0:T(8,128)}, f32[2,16,2]{2,1,0:T(8,128)S(1)}) custom-call(s32[1,1]{1,0:T(1,128)} %bitcast.9.live_ref, f32[256,128]{1,0:T(8,128)S(1)} %bitcast.11, f32[128,256]{1,0:T(8,128)S(1)} %get-tuple-element.17.stiff_ref, f32[128,128]{1,0:T(8,128)S(1)} %get-tuple-element.18.basis_ref), custom_call_target="tpu_custom_call" | custom-call | flops 1000000000 | tf_op jit(solution)/shard_map/blades/pallas_call | solution.py:386
  43.2 8.8 %all-to-all-start.1 = ((f32[64,4,128]{2,1,0:T(4,128)}), f32[64,4,128]{2,1,0:T(4,128)S(1)}, u32[]{:S(2)}, u32[]{:S(2)}) async-start(f32[64,4,128]{2,1,0:T(4,128)} %bitcast.7), calls=%async_computation.1 | async-start | bytes 262144 | tf_op jit(solution)/shard_map/all_to_all | solution.py:395
  52.1 0.0 collective-permute-done.1.low_ref
  52.1 0.0 collective-permute-done.2.high_ref
  52.1 0.0 copy-start.2
  52.1 0.0 copy-start.3
  52.1 0.1 maximum_add_fusion
  52.2 4.5 %collective-permute-start.3 = (f32[2,16,2]{2,1,0:T(8,128)S(1)}, f32[2,16,2]{2,1,0:T(8,128)S(1)}, u32[]{:S(2)}, u32[]{:S(2)}) collective-permute-start(f32[2,16,2]{2,1,0:T(8,128)S(1)} %maximum_add_fusion), channel_id=1, source_target_pairs={{0,256},{8,264},{16,272},{24,280},{32,288},{40,296},{48,304},{56,3... | collective-permute-start | bytes 776 | tf_op jit(solution)/shard_map/ppermute | solution.py:396
  56.7 0.0 collective-permute-done.p_ref
  56.7 0.0 copy-done
  56.7 0.0 copy-done.2
  56.7 0.0 copy-done.3
  56.8 5.0 %adjust.1 = (f32[32,16]{1,0:T(8,128)S(1)}, f32[64,1152]{1,0:T(8,128)S(1)}) custom-call(s32[64]{0:T(128)S(1)} %copy-done.4, s32[1024]{0:T(1024)S(1)} %copy-done.3, f32[64,128]{1,0:T(8,128)S(1)} %bitcast.13, f32[2,16,8192]{2,1,0:T(8,128)S(1)} %copy-done, f32[2,16,8192]{2,1,0:T(8,128)S(1)} %collective-permute-done.p_ref), custom_call_target="tpu_custom_call" | custom-call | flops 40000000000 | tf_op jit(solution)/shard_map/adjust/pallas_call | solution.py:399
  61.7 0.0 collective-permute-done.3.p_edge_ref
  61.7 4.8 %all-to-all-done.1 = f32[64,4,128]{2,1,0:T(4,128)S(1)} async-done(((f32[64,4,128]{2,1,0:T(4,128)}), f32[64,4,128]{2,1,0:T(4,128)S(1)}, u32[]{:S(2)}, u32[]{:S(2)}) %all-to-all-start.1) | async-done | bytes 131104 | tf_op jit(solution)/shard_map/all_to_all | solution.py:395
  66.5 0.9 cross.1
  67.4 0.1 broadcast_in_dim.6
  67.5 15.9 %all_to_all.20 = f32[32,4,128]{2,1,0:T(4,128)S(1)} all-to-all(f32[32,4,128]{2,1,0:T(4,128)S(1)} %broadcast_in_dim.14), channel_id=1, replica_groups=mesh['y'=4,'z'=16,'x'=4,'core'=2] {'y','x','core'}, dimensions={0} | all-to-all | bytes 131072 | tf_op jit(solution)/shard_map/all_to_all | solution.py:333
  83.5 0.6 broadcast_in_dim.15
  84.1 4.2 %all-to-all-start.3 = ((f32[16,4,128]{2,1,0:T(4,128)}), f32[16,4,128]{2,1,0:T(4,128)S(1)}, u32[]{:S(2)}, u32[]{:S(2)}) async-start(f32[16,4,128]{2,1,0:T(4,128)} %broadcast_in_dim.15), calls=%async_computation.3 | async-start | bytes 65536 | tf_op jit(solution)/shard_map/all_to_all | solution.py:333
  88.3 6.0 %image.1 = f32[2,16,8192]{2,1,0:T(8,128)} custom-call(s32[64]{0:T(128)S(1)} %copy-done.4, s32[1,1024]{1,0:T(1,128)S(1)} %bitcast.16, f32[64,128]{1,0:T(8,128)S(1)} %bitcast.14, f32[2,16,8192]{2,1,0:T(8,128)S(1)} %copy-done, f32[2,16,8192]{2,1,0:T(8,128)S(1)} %collective-permute-done.p_ref, f32[2,16,1]{2,1,0:T(8,128)S(1)} %collective-permute-done.1.low_ref, ...), custom_call_target="tpu_custom_call" | custom-call | flops 20000000000 | tf_op jit(solution)/shard_map/image/pallas_call | solution.py:425
  94.3 5.4 %all-to-all-done.3 = f32[16,4,128]{2,1,0:T(4,128)S(1)} async-done(((f32[16,4,128]{2,1,0:T(4,128)}), f32[16,4,128]{2,1,0:T(4,128)S(1)}, u32[]{:S(2)}, u32[]{:S(2)}) %all-to-all-start.3) | async-done | bytes 32800 | tf_op jit(solution)/shard_map/all_to_all | solution.py:333
  99.8 0.7 reshape.46
  (3 shorter events, 0.1 us)
Async XLA Ops:
  0.6 33.7 %copy-start.1 = (f32[128,1,1024]{2,1,0:T(1,128)S(1)}, f32[128,1,1024]{2,1,0:T(1,128)}, u32[]{:S(2)}) copy-start(f32[128,1,1024]{2,1,0:T(1,128)} %param.11) | copy-start | bytes 1572868
  0.6 56.1 %collective-permute-start = (f32[2,16,8192]{2,1,0:T(8,128)}, f32[2,16,8192]{2,1,0:T(8,128)S(1)}, u32[]{:S(2)}, u32[]{:S(2)}) collective-permute-start(f32[2,16,8192]{2,1,0:T(8,128)} %v_ref.3), channel_id=1, source_target_pairs={{0,256},{8,264},{16,272},{24,280},{32,288},{40,296},{48,304},{56,3... | collective-permute-start | bytes 3145736 | tf_op jit(solution)/shard_map/ppermute | solution.py:346
  11.1 16.4 %copy-start.6 = (f32[2,16,1]{2,1,0:T(8,128)S(1)}, f32[2,16,1]{2,1,0:T(8,128)}, u32[]{:S(2)}) copy-start(f32[2,16,1]{2,1,0:T(8,128)} %get-tuple-element.14) | copy-start | bytes 388
  11.2 20.6 %copy-start.5 = (f32[2,16,1]{2,1,0:T(8,128)S(1)}, f32[2,16,1]{2,1,0:T(8,128)}, u32[]{:S(2)}) copy-start(f32[2,16,1]{2,1,0:T(8,128)} %get-tuple-element.15) | copy-start | bytes 388
  11.2 30.3 %all-to-all-start = ((f32[64,4,128]{2,1,0:T(4,128)}), f32[64,4,128]{2,1,0:T(4,128)S(1)}, u32[]{:S(2)}, u32[]{:S(2)}) async-start(f32[64,4,128]{2,1,0:T(4,128)} %bitcast.18), calls=%async_computation | async-start | bytes 262144 | tf_op jit(solution)/shard_map/all_to_all | solution.py:368
  27.5 24.6 %collective-permute-start.1 = (f32[2,16,1]{2,1,0:T(8,128)S(1)}, f32[2,16,1]{2,1,0:T(8,128)S(1)}, u32[]{:S(2)}, u32[]{:S(2)}) collective-permute-start(f32[2,16,1]{2,1,0:T(8,128)S(1)} %copy-done.6), channel_id=1, source_target_pairs={{0,1},{1,2},{2,3},{3,4},{4,5},{5,6},{6,7},{8,9},{9,10},{10,11},{11... | collective-permute-start | bytes 392 | tf_op jit(solution)/shard_map/ppermute | solution.py:370
  31.8 20.3 %collective-permute-start.2 = (f32[2,16,1]{2,1,0:T(8,128)S(1)}, f32[2,16,1]{2,1,0:T(8,128)S(1)}, u32[]{:S(2)}, u32[]{:S(2)}) collective-permute-start(f32[2,16,1]{2,1,0:T(8,128)S(1)} %copy-done.5), channel_id=1, source_target_pairs={{1,0},{2,1},{3,2},{4,3},{5,4},{6,5},{7,6},{9,8},{10,9},{11,10},{12... | collective-permute-start | bytes 392 | tf_op jit(solution)/shard_map/ppermute | solution.py:371
  34.3 0.7 copy-start.4
  41.5 15.3 %copy-start = (f32[2,16,8192]{2,1,0:T(8,128)S(1)}, f32[2,16,8192]{2,1,0:T(8,128)}, u32[]{:S(2)}) copy-start(f32[2,16,8192]{2,1,0:T(8,128)} %v_ref.3) | copy-start | bytes 3145732
  43.2 23.3 %all-to-all-start.1 = ((f32[64,4,128]{2,1,0:T(4,128)}), f32[64,4,128]{2,1,0:T(4,128)S(1)}, u32[]{:S(2)}, u32[]{:S(2)}) async-start(f32[64,4,128]{2,1,0:T(4,128)} %bitcast.7), calls=%async_computation.1 | async-start | bytes 262144 | tf_op jit(solution)/shard_map/all_to_all | solution.py:395
  52.1 4.6 %copy-start.2 = (f32[8192]{0:T(1024)S(1)}, f32[8192]{0:T(1024)}, u32[]{:S(2)}) copy-start(f32[8192]{0:T(1024)} %param.7) | copy-start | bytes 98308
  52.1 4.6 %copy-start.3 = (s32[1024]{0:T(1024)S(1)}, s32[1024]{0:T(1024)}, u32[]{:S(2)}) copy-start(s32[1024]{0:T(1024)} %attach_ref.1) | copy-start | bytes 12292
  52.2 9.5 %collective-permute-start.3 = (f32[2,16,2]{2,1,0:T(8,128)S(1)}, f32[2,16,2]{2,1,0:T(8,128)S(1)}, u32[]{:S(2)}, u32[]{:S(2)}) collective-permute-start(f32[2,16,2]{2,1,0:T(8,128)S(1)} %maximum_add_fusion), channel_id=1, source_target_pairs={{0,256},{8,264},{16,272},{24,280},{32,288},{40,296},{48,304},{56,3... | collective-permute-start | bytes 776 | tf_op jit(solution)/shard_map/ppermute | solution.py:396
  84.1 15.7 %all-to-all-start.3 = ((f32[16,4,128]{2,1,0:T(4,128)}), f32[16,4,128]{2,1,0:T(4,128)S(1)}, u32[]{:S(2)}, u32[]{:S(2)}) async-start(f32[16,4,128]{2,1,0:T(4,128)} %broadcast_in_dim.15), calls=%async_computation.3 | async-start | bytes 65536 | tf_op jit(solution)/shard_map/all_to_all | solution.py:333
